TPU v7x, 256 devices: a whole 4x4x8 slice. The times are simulated.
256 devices in a mesh: ctx: 64 (over z, y_lo, x), head: 4 (over y_hi, core).
Axes of the slice: x: 4, y: 4 (y_hi: 2, y_lo: 2; y = y_hi * 2 + y_lo), z: 8, core: 2. Of those that a mesh axis runs over, the one named last changes fastest.
Arguments:
- rotated_queries: bfloat16 [16384, 4096], P('ctx', 'head')
- rotated_keys: bfloat16 [16384, 512], P('ctx', 'head')
- projected_values: bfloat16 [16384, 512], P('ctx', 'head'), may hold values from -6 to 6
- doc_ids: int32 [16384], P('ctx'), may hold values from 0 to 15, never falling along the last dimension, each value on 1 to 2048 neighbouring positions
- w_out: bfloat16 [4096, 2560], P('head'), may hold values from -0.125 to 0.125
Outputs:
- mixed_out: bfloat16 [16384, 2560], P('ctx', 'head')
Inputs may be any that keep to these rules, and one draw needn't show every extreme that they name: `doc_ids`: document numbers never fall along the pack; each document has at most 2048 tokens, and one has exactly 2048.
All inputs are finite; a program needn't handle non-finite values.
Results may differ from a plain program's by a relative error of at most 0.014.
Values may be sent and summed in bfloat16 or wider, within the bound.
A program may use at most 320 MiB of HBM per device.

v0:
```python
import math

import jax
import jax.numpy as jnp
from jax import lax
from jax.sharding import PartitionSpec as P

QUERY_HEADS = 32
KEY_VALUE_HEADS = 4
HEAD_SIZE = 128
MAXDOC = 2048


masked_value = -1e30


def from_behind(block, axis, distance):
    devices = range(lax.axis_size(axis))
    route = [(i - distance, i) for i in devices if i - distance in devices]
    return lax.ppermute(block, axis, route)


def local(rotated_queries, rotated_keys, projected_values, doc_ids, w_out):
    rows_dev = rotated_queries.shape[0]
    kv_heads = rotated_keys.shape[1] // HEAD_SIZE
    query_group = QUERY_HEADS // KEY_VALUE_HEADS
    score_scale = 1.0 / math.sqrt(HEAD_SIZE)
    query_rows = rotated_queries.reshape(rows_dev, kv_heads, query_group, HEAD_SIZE)
    doc_marks = doc_ids + 1
    query_pos = jnp.arange(rows_dev, dtype=jnp.int32)
    window = MAXDOC // rows_dev + 1

    def attend(state, key_block, value_block, key_marks, key_pos):
        run_max, run_sum, run_acc = state
        count = key_block.shape[0]
        key_rows = key_block.reshape(count, kv_heads, HEAD_SIZE)
        value_rows = value_block.reshape(count, kv_heads, HEAD_SIZE)
        scores = (
            jnp.einsum("tkgd,skd->kgts", query_rows, key_rows, preferred_element_type=jnp.float32)
            * score_scale
        )
        visible = (key_marks[None, :] == doc_marks[:, None]) & (
            key_pos[None, :] <= query_pos[:, None]
        )
        scores = jnp.where(visible, scores, masked_value)
        new_max = jnp.maximum(run_max, jnp.max(scores, axis=-1))
        weights = jnp.where(visible, jnp.exp(scores - new_max[..., None]), 0.0)
        factor = jnp.exp(run_max - new_max)
        run_sum = run_sum * factor + jnp.sum(weights, axis=-1)
        update = jnp.einsum(
            "kgts,skd->kgtd",
            weights.astype(jnp.bfloat16),
            value_rows,
            preferred_element_type=jnp.float32,
        )
        run_acc = run_acc * factor[..., None] + update
        return (new_max, run_sum, run_acc)

    def guarded(state, key_block, value_block, key_marks, key_pos):
        return attend(state, key_block, value_block, key_marks, key_pos)

    state = (
        jnp.full((kv_heads, query_group, rows_dev), masked_value, jnp.float32),
        jnp.zeros((kv_heads, query_group, rows_dev), jnp.float32),
        jnp.zeros((kv_heads, query_group, rows_dev, HEAD_SIZE), jnp.float32),
    )
    state = guarded(state, rotated_keys, projected_values, doc_marks, query_pos)

    def advance(stop, carry):
        current, inner = carry
        current = from_behind((current[0], current[1], current[2]), "ctx", 1)
        key_pos = query_pos - (stop + 1) * rows_dev
        return (current, guarded(inner, current[0], current[1], current[2], key_pos))

    _, state = lax.fori_loop(
        0, window - 1, advance, ((rotated_keys, projected_values, doc_marks), state)
    )
    run_max, run_sum, run_acc = state
    attended = (
        (run_acc / run_sum[..., None])
        .transpose(2, 0, 1, 3)
        .reshape(rows_dev, kv_heads * query_group * HEAD_SIZE)
        .astype(jnp.bfloat16)
    )
    partial_value = jnp.dot(attended, w_out, preferred_element_type=jnp.float32).astype(
        jnp.bfloat16
    )
    return (
        lax.psum_scatter(partial_value, "head", scatter_dimension=1, tiled=True)
        .astype(jnp.float32)
        .astype(jnp.bfloat16)
    )


def solution(mesh):
    placed = (P("ctx", "head"), P("ctx", "head"), P("ctx", "head"), P("ctx"), P("head", None))
    return jax.shard_map(
        local, mesh=mesh, in_specs=placed, out_specs=P("ctx", "head"), check_vma=False
    )
```

profile of v0, /device:TPU:128, one launch (start us, length us, event | category | flops | bytes accessed | tf_op | source)
XLA Modules:
  0.0 201.0 jit_solution(2930337731464363341)
XLA Ops:
  9.0 1.2 copy.18
  10.3 1.5 fusion.22
  12.6 1.9 fusion.25
  14.5 132.8 %while.25 = (s32[]{:T(128)}, bf16[256,128]{1,0:T(8,128)(2,1)S(1)}, bf16[256,128]{1,0:T(8,128)(2,1)S(1)}, s32[256]{0:T(256)S(1)}, f32[1,8,256]{2,1,0:T(8,128)S(1)...) while((s32[]{:T(128)}, bf16[256,128]{1,0:T(8,128)(2,1)S(1)}, ...), condition=%wide.region_5.6_spmd.clone.clone, body=%wide.region_2.5_spmd.clone.clone.sunk | while | flops 275978496 | bytes 18622764 | solution.py:75
  14.5 3.4 %collective-permute-start.2 = (s32[256]{0:T(256)S(1)}, s32[256]{0:T(256)S(1)}, u32[]{:S(2)}, u32[]{:S(2)}) collective-permute-start(s32[256]{0:T(256)S(1)} %get-tuple-element.346), channel_id=1, source_target_pairs={{0,4},{4,8},{8,12},{12,16},{16,20},{20,24},{24,28},{28,32},{32,36}... | collective-permute-start | bytes 3080 | tf_op jit(solution)/shard_map/while/body/eval_jaxpr/ppermute | solution.py:20
  17.9 3.4 %collective-permute-start = (bf16[256,128]{1,0:T(8,128)(2,1)S(1)}, bf16[256,128]{1,0:T(8,128)(2,1)S(1)}, u32[]{:S(2)}, u32[]{:S(2)}) collective-permute-start(bf16[256,128]{1,0:T(8,128)(2,1)S(1)} %get-tuple-element.344), channel_id=1, source_target_pairs={{0,4},{4,8},{8,12},{12,16},{16,20},{20,24},{24,28},{28,32},{32,36}... | collective-permute-start | bytes 196616 | tf_op jit(solution)/shard_map/while/body/eval_jaxpr/ppermute | solution.py:20
  21.3 3.1 %collective-permute-start.1 = (bf16[256,128]{1,0:T(8,128)(2,1)S(1)}, bf16[256,128]{1,0:T(8,128)(2,1)S(1)}, u32[]{:S(2)}, u32[]{:S(2)}) collective-permute-start(bf16[256,128]{1,0:T(8,128)(2,1)S(1)} %get-tuple-element.345), channel_id=1, source_target_pairs={{0,4},{4,8},{8,12},{12,16},{16,20},{20,24},{24,28},{28,32},{32,36}... | collective-permute-start | bytes 196616 | tf_op jit(solution)/shard_map/while/body/eval_jaxpr/ppermute | solution.py:20
  24.6 3.7 %collective-permute-done = bf16[256,128]{1,0:T(8,128)(2,1)S(1)} collective-permute-done((bf16[256,128]{1,0:T(8,128)(2,1)S(1)}, bf16[256,128]{1,0:T(8,128)(2,1)S(1)}, u32[]{:S(2)}, u32[]{:S(2)}) %collective-permute-start) | collective-permute-done | bytes 65568 | tf_op jit(solution)/shard_map/while/body/eval_jaxpr/ppermute | solution.py:20
  29.3 2.4 %collective-permute-done.1 = bf16[256,128]{1,0:T(8,128)(2,1)S(1)} collective-permute-done((bf16[256,128]{1,0:T(8,128)(2,1)S(1)}, bf16[256,128]{1,0:T(8,128)(2,1)S(1)}, u32[]{:S(2)}, u32[]{:S(2)}) %collective-permute-start.1) | collective-permute-done | bytes 65568 | tf_op jit(solution)/shard_map/while/body/eval_jaxpr/ppermute | solution.py:20
  31.7 1.0 fusion.59
  32.7 1.0 copy-done.1
  33.7 1.9 collective-permute-start.2
  35.6 1.9 collective-permute-start
  37.5 1.9 collective-permute-start.1
  39.5 3.9 %collective-permute-done.2 = s32[256]{0:T(256)S(1)} collective-permute-done((s32[256]{0:T(256)S(1)}, s32[256]{0:T(256)S(1)}, u32[]{:S(2)}, u32[]{:S(2)}) %collective-permute-start.2) | collective-permute-done | bytes 1056 | tf_op jit(solution)/shard_map/while/body/eval_jaxpr/ppermute | solution.py:20
  43.5 2.5 %collective-permute-done = bf16[256,128]{1,0:T(8,128)(2,1)S(1)} collective-permute-done((bf16[256,128]{1,0:T(8,128)(2,1)S(1)}, bf16[256,128]{1,0:T(8,128)(2,1)S(1)}, u32[]{:S(2)}, u32[]{:S(2)}) %collective-permute-start) | collective-permute-done | bytes 65568 | tf_op jit(solution)/shard_map/while/body/eval_jaxpr/ppermute | solution.py:20
  47.9 1.0 fusion.59
  48.9 1.0 copy-done.1
  49.9 1.9 collective-permute-start.2
  51.8 1.9 collective-permute-start
  53.8 1.9 collective-permute-start.1
  55.7 3.9 %collective-permute-done.2 = s32[256]{0:T(256)S(1)} collective-permute-done((s32[256]{0:T(256)S(1)}, s32[256]{0:T(256)S(1)}, u32[]{:S(2)}, u32[]{:S(2)}) %collective-permute-start.2) | collective-permute-done | bytes 1056 | tf_op jit(solution)/shard_map/while/body/eval_jaxpr/ppermute | solution.py:20
  59.7 2.5 %collective-permute-done = bf16[256,128]{1,0:T(8,128)(2,1)S(1)} collective-permute-done((bf16[256,128]{1,0:T(8,128)(2,1)S(1)}, bf16[256,128]{1,0:T(8,128)(2,1)S(1)}, u32[]{:S(2)}, u32[]{:S(2)}) %collective-permute-start) | collective-permute-done | bytes 65568 | tf_op jit(solution)/shard_map/while/body/eval_jaxpr/ppermute | solution.py:20
  64.1 1.0 fusion.59
  65.2 1.0 copy-done.1
  66.1 1.9 collective-permute-start.2
  68.1 1.9 collective-permute-start
  70.0 1.9 collective-permute-start.1
  71.9 3.9 %collective-permute-done.2 = s32[256]{0:T(256)S(1)} collective-permute-done((s32[256]{0:T(256)S(1)}, s32[256]{0:T(256)S(1)}, u32[]{:S(2)}, u32[]{:S(2)}) %collective-permute-start.2) | collective-permute-done | bytes 1056 | tf_op jit(solution)/shard_map/while/body/eval_jaxpr/ppermute | solution.py:20
  76.0 2.5 %collective-permute-done = bf16[256,128]{1,0:T(8,128)(2,1)S(1)} collective-permute-done((bf16[256,128]{1,0:T(8,128)(2,1)S(1)}, bf16[256,128]{1,0:T(8,128)(2,1)S(1)}, u32[]{:S(2)}, u32[]{:S(2)}) %collective-permute-start) | collective-permute-done | bytes 65568 | tf_op jit(solution)/shard_map/while/body/eval_jaxpr/ppermute | solution.py:20
  80.4 1.0 fusion.59
  81.4 1.0 copy-done.1
  82.4 1.9 collective-permute-start.2
  84.3 1.9 collective-permute-start
  86.2 1.9 collective-permute-start.1
  88.2 3.9 %collective-permute-done.2 = s32[256]{0:T(256)S(1)} collective-permute-done((s32[256]{0:T(256)S(1)}, s32[256]{0:T(256)S(1)}, u32[]{:S(2)}, u32[]{:S(2)}) %collective-permute-start.2) | collective-permute-done | bytes 1056 | tf_op jit(solution)/shard_map/while/body/eval_jaxpr/ppermute | solution.py:20
  92.2 2.5 %collective-permute-done = bf16[256,128]{1,0:T(8,128)(2,1)S(1)} collective-permute-done((bf16[256,128]{1,0:T(8,128)(2,1)S(1)}, bf16[256,128]{1,0:T(8,128)(2,1)S(1)}, u32[]{:S(2)}, u32[]{:S(2)}) %collective-permute-start) | collective-permute-done | bytes 65568 | tf_op jit(solution)/shard_map/while/body/eval_jaxpr/ppermute | solution.py:20
  96.6 1.0 fusion.59
  97.6 1.0 copy-done.1
  98.6 1.9 collective-permute-start.2
  100.5 1.9 collective-permute-start
  102.4 1.9 collective-permute-start.1
  104.4 3.9 %collective-permute-done.2 = s32[256]{0:T(256)S(1)} collective-permute-done((s32[256]{0:T(256)S(1)}, s32[256]{0:T(256)S(1)}, u32[]{:S(2)}, u32[]{:S(2)}) %collective-permute-start.2) | collective-permute-done | bytes 1056 | tf_op jit(solution)/shard_map/while/body/eval_jaxpr/ppermute | solution.py:20
  108.4 2.5 %collective-permute-done = bf16[256,128]{1,0:T(8,128)(2,1)S(1)} collective-permute-done((bf16[256,128]{1,0:T(8,128)(2,1)S(1)}, bf16[256,128]{1,0:T(8,128)(2,1)S(1)}, u32[]{:S(2)}, u32[]{:S(2)}) %collective-permute-start) | collective-permute-done | bytes 65568 | tf_op jit(solution)/shard_map/while/body/eval_jaxpr/ppermute | solution.py:20
  112.8 1.0 fusion.59
  113.8 1.0 copy-done.1
  114.8 1.9 collective-permute-start.2
  116.7 1.9 collective-permute-start
  118.7 1.9 collective-permute-start.1
  120.6 3.9 %collective-permute-done.2 = s32[256]{0:T(256)S(1)} collective-permute-done((s32[256]{0:T(256)S(1)}, s32[256]{0:T(256)S(1)}, u32[]{:S(2)}, u32[]{:S(2)}) %collective-permute-start.2) | collective-permute-done | bytes 1056 | tf_op jit(solution)/shard_map/while/body/eval_jaxpr/ppermute | solution.py:20
  124.6 2.5 %collective-permute-done = bf16[256,128]{1,0:T(8,128)(2,1)S(1)} collective-permute-done((bf16[256,128]{1,0:T(8,128)(2,1)S(1)}, bf16[256,128]{1,0:T(8,128)(2,1)S(1)}, u32[]{:S(2)}, u32[]{:S(2)}) %collective-permute-start) | collective-permute-done | bytes 65568 | tf_op jit(solution)/shard_map/while/body/eval_jaxpr/ppermute | solution.py:20
  129.1 1.0 fusion.59
  130.1 1.0 copy-done.1
  131.1 1.9 collective-permute-start.2
  133.0 1.9 collective-permute-start
  134.9 1.9 collective-permute-start.1
  136.8 3.9 %collective-permute-done.2 = s32[256]{0:T(256)S(1)} collective-permute-done((s32[256]{0:T(256)S(1)}, s32[256]{0:T(256)S(1)}, u32[]{:S(2)}, u32[]{:S(2)}) %collective-permute-start.2) | collective-permute-done | bytes 1056 | tf_op jit(solution)/shard_map/while/body/eval_jaxpr/ppermute | solution.py:20
  140.9 2.5 %collective-permute-done = bf16[256,128]{1,0:T(8,128)(2,1)S(1)} collective-permute-done((bf16[256,128]{1,0:T(8,128)(2,1)S(1)}, bf16[256,128]{1,0:T(8,128)(2,1)S(1)}, u32[]{:S(2)}, u32[]{:S(2)}) %collective-permute-start) | collective-permute-done | bytes 65568 | tf_op jit(solution)/shard_map/while/body/eval_jaxpr/ppermute | solution.py:20
  145.3 1.0 fusion.59
  147.3 1.6 copy.20
  149.0 4.0 %convolution_convert_fusion = bf16[256,2560]{1,0:T(8,128)(2,1)S(1)} fusion(bf16[256,1024]{0,1:T(8,128)(2,1)S(1)} %bitcast.120, bf16[1024,2560]{1,0:T(8,128)(2,1)} %param.11), kind=kOutput, calls=%fused_computation.28 | convolution fusion | flops 1342832640 | bytes 7077888 | tf_op jit(solution)/shard_map/dot_general | solution.py:85
  153.0 1.5 copy.23
  154.5 37.8 %reduce-scatter.4.cloned.1.call-done = bf16[640,256]{1,0:T(8,128)(2,1)} async-done(((bf16[2560,256]{1,0:T(8,128)(2,1)}), bf16[640,256]{1,0:T(8,128)(2,1)}) %reduce-scatter.4.cloned.1.call-update) | async-done | bytes 327696
  192.3 1.9 copy.24
  (125 shorter events, 19.8 us)
Async XLA Ops:
  6.5 185.8 %reduce-scatter.4.cloned.1.call-start = ((), (), s32[]{:S(2)}) async-start(), calls=%async_computation.1 | async-start | bytes 1638400
  14.5 9.9 %collective-permute-start.2 = (s32[256]{0:T(256)S(1)}, s32[256]{0:T(256)S(1)}, u32[]{:S(2)}, u32[]{:S(2)}) collective-permute-start(s32[256]{0:T(256)S(1)} %get-tuple-element.346), channel_id=1, source_target_pairs={{0,4},{4,8},{8,12},{12,16},{16,20},{20,24},{24,28},{28,32},{32,36}... | collective-permute-start | bytes 3080 | tf_op jit(solution)/shard_map/while/body/eval_jaxpr/ppermute | solution.py:20
  17.9 10.4 %collective-permute-start = (bf16[256,128]{1,0:T(8,128)(2,1)S(1)}, bf16[256,128]{1,0:T(8,128)(2,1)S(1)}, u32[]{:S(2)}, u32[]{:S(2)}) collective-permute-start(bf16[256,128]{1,0:T(8,128)(2,1)S(1)} %get-tuple-element.344), channel_id=1, source_target_pairs={{0,4},{4,8},{8,12},{12,16},{16,20},{20,24},{24,28},{28,32},{32,36}... | collective-permute-start | bytes 196616 | tf_op jit(solution)/shard_map/while/body/eval_jaxpr/ppermute | solution.py:20
  21.3 10.4 %collective-permute-start.1 = (bf16[256,128]{1,0:T(8,128)(2,1)S(1)}, bf16[256,128]{1,0:T(8,128)(2,1)S(1)}, u32[]{:S(2)}, u32[]{:S(2)}) collective-permute-start(bf16[256,128]{1,0:T(8,128)(2,1)S(1)} %get-tuple-element.345), channel_id=1, source_target_pairs={{0,4},{4,8},{8,12},{12,16},{16,20},{20,24},{24,28},{28,32},{32,36}... | collective-permute-start | bytes 196616 | tf_op jit(solution)/shard_map/while/body/eval_jaxpr/ppermute | solution.py:20
  28.3 3.4 %copy-start = (f32[1,8,256,128]{3,2,1,0:T(8,128)S(1)}, f32[1,8,256,128]{3,2,1,0:T(8,128)}, u32[]{:S(2)}) copy-start(f32[1,8,256,128]{3,2,1,0:T(8,128)} %get-tuple-element.349) | copy-start | bytes 3145732 | tf_op jit(solution)/shard_map/while
  32.7 1.0 copy-start.1
  33.7 9.7 %collective-permute-start.2 = (s32[256]{0:T(256)S(1)}, s32[256]{0:T(256)S(1)}, u32[]{:S(2)}, u32[]{:S(2)}) collective-permute-start(s32[256]{0:T(256)S(1)} %get-tuple-element.346), channel_id=1, source_target_pairs={{0,4},{4,8},{8,12},{12,16},{16,20},{20,24},{24,28},{28,32},{32,36}... | collective-permute-start | bytes 3080 | tf_op jit(solution)/shard_map/while/body/eval_jaxpr/ppermute | solution.py:20
  35.6 10.4 %collective-permute-start = (bf16[256,128]{1,0:T(8,128)(2,1)S(1)}, bf16[256,128]{1,0:T(8,128)(2,1)S(1)}, u32[]{:S(2)}, u32[]{:S(2)}) collective-permute-start(bf16[256,128]{1,0:T(8,128)(2,1)S(1)} %get-tuple-element.344), channel_id=1, source_target_pairs={{0,4},{4,8},{8,12},{12,16},{16,20},{20,24},{24,28},{28,32},{32,36}... | collective-permute-start | bytes 196616 | tf_op jit(solution)/shard_map/while/body/eval_jaxpr/ppermute | solution.py:20
  37.5 10.4 %collective-permute-start.1 = (bf16[256,128]{1,0:T(8,128)(2,1)S(1)}, bf16[256,128]{1,0:T(8,128)(2,1)S(1)}, u32[]{:S(2)}, u32[]{:S(2)}) collective-permute-start(bf16[256,128]{1,0:T(8,128)(2,1)S(1)} %get-tuple-element.345), channel_id=1, source_target_pairs={{0,4},{4,8},{8,12},{12,16},{16,20},{20,24},{24,28},{28,32},{32,36}... | collective-permute-start | bytes 196616 | tf_op jit(solution)/shard_map/while/body/eval_jaxpr/ppermute | solution.py:20
  46.0 1.9 copy-start
  48.9 1.0 copy-start.1
  49.9 9.7 %collective-permute-start.2 = (s32[256]{0:T(256)S(1)}, s32[256]{0:T(256)S(1)}, u32[]{:S(2)}, u32[]{:S(2)}) collective-permute-start(s32[256]{0:T(256)S(1)} %get-tuple-element.346), channel_id=1, source_target_pairs={{0,4},{4,8},{8,12},{12,16},{16,20},{20,24},{24,28},{28,32},{32,36}... | collective-permute-start | bytes 3080 | tf_op jit(solution)/shard_map/while/body/eval_jaxpr/ppermute | solution.py:20
  51.8 10.4 %collective-permute-start = (bf16[256,128]{1,0:T(8,128)(2,1)S(1)}, bf16[256,128]{1,0:T(8,128)(2,1)S(1)}, u32[]{:S(2)}, u32[]{:S(2)}) collective-permute-start(bf16[256,128]{1,0:T(8,128)(2,1)S(1)} %get-tuple-element.344), channel_id=1, source_target_pairs={{0,4},{4,8},{8,12},{12,16},{16,20},{20,24},{24,28},{28,32},{32,36}... | collective-permute-start | bytes 196616 | tf_op jit(solution)/shard_map/while/body/eval_jaxpr/ppermute | solution.py:20
  53.8 10.4 %collective-permute-start.1 = (bf16[256,128]{1,0:T(8,128)(2,1)S(1)}, bf16[256,128]{1,0:T(8,128)(2,1)S(1)}, u32[]{:S(2)}, u32[]{:S(2)}) collective-permute-start(bf16[256,128]{1,0:T(8,128)(2,1)S(1)} %get-tuple-element.345), channel_id=1, source_target_pairs={{0,4},{4,8},{8,12},{12,16},{16,20},{20,24},{24,28},{28,32},{32,36}... | collective-permute-start | bytes 196616 | tf_op jit(solution)/shard_map/while/body/eval_jaxpr/ppermute | solution.py:20
  62.2 1.9 copy-start
  65.1 1.0 copy-start.1
  66.1 9.7 %collective-permute-start.2 = (s32[256]{0:T(256)S(1)}, s32[256]{0:T(256)S(1)}, u32[]{:S(2)}, u32[]{:S(2)}) collective-permute-start(s32[256]{0:T(256)S(1)} %get-tuple-element.346), channel_id=1, source_target_pairs={{0,4},{4,8},{8,12},{12,16},{16,20},{20,24},{24,28},{28,32},{32,36}... | collective-permute-start | bytes 3080 | tf_op jit(solution)/shard_map/while/body/eval_jaxpr/ppermute | solution.py:20
  68.1 10.4 %collective-permute-start = (bf16[256,128]{1,0:T(8,128)(2,1)S(1)}, bf16[256,128]{1,0:T(8,128)(2,1)S(1)}, u32[]{:S(2)}, u32[]{:S(2)}) collective-permute-start(bf16[256,128]{1,0:T(8,128)(2,1)S(1)} %get-tuple-element.344), channel_id=1, source_target_pairs={{0,4},{4,8},{8,12},{12,16},{16,20},{20,24},{24,28},{28,32},{32,36}... | collective-permute-start | bytes 196616 | tf_op jit(solution)/shard_map/while/body/eval_jaxpr/ppermute | solution.py:20
  70.0 10.4 %collective-permute-start.1 = (bf16[256,128]{1,0:T(8,128)(2,1)S(1)}, bf16[256,128]{1,0:T(8,128)(2,1)S(1)}, u32[]{:S(2)}, u32[]{:S(2)}) collective-permute-start(bf16[256,128]{1,0:T(8,128)(2,1)S(1)} %get-tuple-element.345), channel_id=1, source_target_pairs={{0,4},{4,8},{8,12},{12,16},{16,20},{20,24},{24,28},{28,32},{32,36}... | collective-permute-start | bytes 196616 | tf_op jit(solution)/shard_map/while/body/eval_jaxpr/ppermute | solution.py:20
  78.4 1.9 copy-start
  81.4 1.0 copy-start.1
  82.4 9.7 %collective-permute-start.2 = (s32[256]{0:T(256)S(1)}, s32[256]{0:T(256)S(1)}, u32[]{:S(2)}, u32[]{:S(2)}) collective-permute-start(s32[256]{0:T(256)S(1)} %get-tuple-element.346), channel_id=1, source_target_pairs={{0,4},{4,8},{8,12},{12,16},{16,20},{20,24},{24,28},{28,32},{32,36}... | collective-permute-start | bytes 3080 | tf_op jit(solution)/shard_map/while/body/eval_jaxpr/ppermute | solution.py:20
  84.3 10.4 %collective-permute-start = (bf16[256,128]{1,0:T(8,128)(2,1)S(1)}, bf16[256,128]{1,0:T(8,128)(2,1)S(1)}, u32[]{:S(2)}, u32[]{:S(2)}) collective-permute-start(bf16[256,128]{1,0:T(8,128)(2,1)S(1)} %get-tuple-element.344), channel_id=1, source_target_pairs={{0,4},{4,8},{8,12},{12,16},{16,20},{20,24},{24,28},{28,32},{32,36}... | collective-permute-start | bytes 196616 | tf_op jit(solution)/shard_map/while/body/eval_jaxpr/ppermute | solution.py:20
  86.2 10.4 %collective-permute-start.1 = (bf16[256,128]{1,0:T(8,128)(2,1)S(1)}, bf16[256,128]{1,0:T(8,128)(2,1)S(1)}, u32[]{:S(2)}, u32[]{:S(2)}) collective-permute-start(bf16[256,128]{1,0:T(8,128)(2,1)S(1)} %get-tuple-element.345), channel_id=1, source_target_pairs={{0,4},{4,8},{8,12},{12,16},{16,20},{20,24},{24,28},{28,32},{32,36}... | collective-permute-start | bytes 196616 | tf_op jit(solution)/shard_map/while/body/eval_jaxpr/ppermute | solution.py:20
  94.7 1.9 copy-start
  97.6 1.0 copy-start.1
  98.6 9.7 %collective-permute-start.2 = (s32[256]{0:T(256)S(1)}, s32[256]{0:T(256)S(1)}, u32[]{:S(2)}, u32[]{:S(2)}) collective-permute-start(s32[256]{0:T(256)S(1)} %get-tuple-element.346), channel_id=1, source_target_pairs={{0,4},{4,8},{8,12},{12,16},{16,20},{20,24},{24,28},{28,32},{32,36}... | collective-permute-start | bytes 3080 | tf_op jit(solution)/shard_map/while/body/eval_jaxpr/ppermute | solution.py:20
  100.5 10.4 %collective-permute-start = (bf16[256,128]{1,0:T(8,128)(2,1)S(1)}, bf16[256,128]{1,0:T(8,128)(2,1)S(1)}, u32[]{:S(2)}, u32[]{:S(2)}) collective-permute-start(bf16[256,128]{1,0:T(8,128)(2,1)S(1)} %get-tuple-element.344), channel_id=1, source_target_pairs={{0,4},{4,8},{8,12},{12,16},{16,20},{20,24},{24,28},{28,32},{32,36}... | collective-permute-start | bytes 196616 | tf_op jit(solution)/shard_map/while/body/eval_jaxpr/ppermute | solution.py:20
  102.4 10.4 %collective-permute-start.1 = (bf16[256,128]{1,0:T(8,128)(2,1)S(1)}, bf16[256,128]{1,0:T(8,128)(2,1)S(1)}, u32[]{:S(2)}, u32[]{:S(2)}) collective-permute-start(bf16[256,128]{1,0:T(8,128)(2,1)S(1)} %get-tuple-element.345), channel_id=1, source_target_pairs={{0,4},{4,8},{8,12},{12,16},{16,20},{20,24},{24,28},{28,32},{32,36}... | collective-permute-start | bytes 196616 | tf_op jit(solution)/shard_map/while/body/eval_jaxpr/ppermute | solution.py:20
  110.9 1.9 copy-start
  113.8 1.0 copy-start.1
  114.8 9.7 %collective-permute-start.2 = (s32[256]{0:T(256)S(1)}, s32[256]{0:T(256)S(1)}, u32[]{:S(2)}, u32[]{:S(2)}) collective-permute-start(s32[256]{0:T(256)S(1)} %get-tuple-element.346), channel_id=1, source_target_pairs={{0,4},{4,8},{8,12},{12,16},{16,20},{20,24},{24,28},{28,32},{32,36}... | collective-permute-start | bytes 3080 | tf_op jit(solution)/shard_map/while/body/eval_jaxpr/ppermute | solution.py:20
  116.7 10.4 %collective-permute-start = (bf16[256,128]{1,0:T(8,128)(2,1)S(1)}, bf16[256,128]{1,0:T(8,128)(2,1)S(1)}, u32[]{:S(2)}, u32[]{:S(2)}) collective-permute-start(bf16[256,128]{1,0:T(8,128)(2,1)S(1)} %get-tuple-element.344), channel_id=1, source_target_pairs={{0,4},{4,8},{8,12},{12,16},{16,20},{20,24},{24,28},{28,32},{32,36}... | collective-permute-start | bytes 196616 | tf_op jit(solution)/shard_map/while/body/eval_jaxpr/ppermute | solution.py:20
  118.7 10.4 %collective-permute-start.1 = (bf16[256,128]{1,0:T(8,128)(2,1)S(1)}, bf16[256,128]{1,0:T(8,128)(2,1)S(1)}, u32[]{:S(2)}, u32[]{:S(2)}) collective-permute-start(bf16[256,128]{1,0:T(8,128)(2,1)S(1)} %get-tuple-element.345), channel_id=1, source_target_pairs={{0,4},{4,8},{8,12},{12,16},{16,20},{20,24},{24,28},{28,32},{32,36}... | collective-permute-start | bytes 196616 | tf_op jit(solution)/shard_map/while/body/eval_jaxpr/ppermute | solution.py:20
  127.1 1.9 copy-start
  130.1 1.0 copy-start.1
  131.1 9.7 %collective-permute-start.2 = (s32[256]{0:T(256)S(1)}, s32[256]{0:T(256)S(1)}, u32[]{:S(2)}, u32[]{:S(2)}) collective-permute-start(s32[256]{0:T(256)S(1)} %get-tuple-element.346), channel_id=1, source_target_pairs={{0,4},{4,8},{8,12},{12,16},{16,20},{20,24},{24,28},{28,32},{32,36}... | collective-permute-start | bytes 3080 | tf_op jit(solution)/shard_map/while/body/eval_jaxpr/ppermute | solution.py:20
  133.0 10.4 %collective-permute-start = (bf16[256,128]{1,0:T(8,128)(2,1)S(1)}, bf16[256,128]{1,0:T(8,128)(2,1)S(1)}, u32[]{:S(2)}, u32[]{:S(2)}) collective-permute-start(bf16[256,128]{1,0:T(8,128)(2,1)S(1)} %get-tuple-element.344), channel_id=1, source_target_pairs={{0,4},{4,8},{8,12},{12,16},{16,20},{20,24},{24,28},{28,32},{32,36}... | collective-permute-start | bytes 196616 | tf_op jit(solution)/shard_map/while/body/eval_jaxpr/ppermute | solution.py:20
  134.9 10.4 %collective-permute-start.1 = (bf16[256,128]{1,0:T(8,128)(2,1)S(1)}, bf16[256,128]{1,0:T(8,128)(2,1)S(1)}, u32[]{:S(2)}, u32[]{:S(2)}) collective-permute-start(bf16[256,128]{1,0:T(8,128)(2,1)S(1)} %get-tuple-element.345), channel_id=1, source_target_pairs={{0,4},{4,8},{8,12},{12,16},{16,20},{20,24},{24,28},{28,32},{32,36}... | collective-permute-start | bytes 196616 | tf_op jit(solution)/shard_map/while/body/eval_jaxpr/ppermute | solution.py:20
  143.3 1.9 copy-start
  146.3 1.0 copy-start.1
Sparse Core Ops, SparseCore 0:
  154.6 37.6 reduce-scatter.3
where the time goes:
time: 205 us; the launch traced here: 201 us
  waiting for transfers between devices  94.5 us (46%)
  starting transfers between devices  50.1 us (24%)
  matrix products  19.1 us (9%)
  local copies, waits for them, and re-layouts  16.1 us (8%)
  between operations  13.5 us (7%)
  other arithmetic  6.8 us (3%)
    ppermute x24, waiting for transfers between devices, from_behind(): return lax.ppermute(block, axis, route)  56.6 us
    ppermute x24, starting transfers between devices, from_behind(): return lax.ppermute(block, axis, route)  50.1 us
    unnamed x2, waiting for transfers between devices  37.8 us
    dot_general x9, matrix products, attend(): jnp.einsum('kgts,skd->kgtd', weights.astype(jnp.bfloat16), value_rows, pr...  9.83 us
    while x64, local copies, waits for them, and re-layouts  8.03 us
    unnamed x7, local copies, waits for them, and re-layouts  6.53 us
    dot_general x9, matrix products, attend(): jnp.einsum('tkgd,skd->kgts', query_rows, key_rows, preferred_element_type...  5.22 us
    reduce_sum x9, other arithmetic, attend(): run_sum = run_sum * factor + jnp.sum(weights, axis=-1)  4.63 us
  transfers between devices with their start and end apart: 25, of which 24 were waited for; matrix products, arithmetic and copies ran while one was open for 5% of the time, Pallas kernels for 0%

commit v1 on v0

v1 whole, which is shorter than its diff:
```python
import functools
import math

import jax
import jax.numpy as jnp
from jax import lax
from jax.experimental import pallas as pl
from jax.experimental.pallas import tpu as pltpu
from jax.sharding import PartitionSpec as P

MESH = pl.DeviceIdType.MESH
HD = 128
ROWS = 256
HEADS = 8
BACK = 8
COLS = 640
HIDDEN = -1e30
RATE = math.log2(math.e) / math.sqrt(HD)
CHUNKS = 4
TOK = ROWS // CHUNKS
MSG = 272


def wide(x, n):
    return jnp.concatenate([x] * n, axis=1)


def kernel(n_ctx, q_hbm, k_ref, v_ref, ids_ref, w_hbm, o_ref,
           q, w, own, got, kaug, vaug, qaug, dmask, acc, top, att, keep,
           core_out, core_in, y_out, y_in,
           load_sem, w_sem, send_sem, recv_sem, cs_sem, cr_sem, ys_sem, yr_sem):
    ctx = lax.axis_index("ctx")
    head = lax.axis_index("head")
    y_hi, core = head // 2, lax.rem(head, 2)
    mate = y_hi * 2 + (1 - core)
    far = (1 - y_hi) * 2 + core

    barrier = pltpu.get_barrier_semaphore()
    for j in range(1, BACK + 1):
        @pl.when(ctx - j >= 0)
        def _():
            pl.semaphore_signal(barrier, inc=1, device_id=(ctx - j, head), device_id_type=MESH)
    pl.semaphore_signal(barrier, inc=1, device_id=(ctx, mate), device_id_type=MESH)
    pl.semaphore_signal(barrier, inc=1, device_id=(ctx, far), device_id_type=MESH)

    q_load = pltpu.make_async_copy(q_hbm, q, load_sem)
    q_load.start()
    w_loads = []
    groups = [(1 - y_hi) * 2 + (1 - core), y_hi * 2 + (1 - core), (1 - y_hi) * 2 + core, y_hi * 2 + core]
    for i, g in enumerate(groups):
        c = pltpu.make_async_copy(
            w_hbm.at[:, pl.ds(pl.multiple_of(g * COLS, 128), COLS)], w.at[:, pl.ds(i * COLS, COLS)], w_sem.at[i])
        c.start()
        w_loads.append(c)

    ids = ids_ref[...].astype(jnp.float32)
    own[0:HD, :] = k_ref[...].T
    own[HD:HD + 16, :] = jnp.broadcast_to(ids, (16, ROWS)).astype(jnp.bfloat16)
    own[HD + 16:, 0:HD] = v_ref[0:HD, :]
    own[HD + 16:, HD:] = v_ref[HD:, :]

    reach = jnp.minimum(n_ctx - 1 - ctx, BACK)
    pl.semaphore_wait(barrier, reach + 2)

    def kv_copy(j):
        return pltpu.make_async_remote_copy(
            src_ref=own, dst_ref=got.at[j - 1], send_sem=send_sem.at[j - 1], recv_sem=recv_sem.at[j - 1],
            device_id=(lax.rem(ctx + j, n_ctx), head), device_id_type=MESH)

    for j in range(1, BACK + 1):
        @pl.when(ctx + j < n_ctx)
        def _():
            kv_copy(j).start()

    ids_col = jnp.broadcast_to(ids, (HD, ROWS)).T
    first = ids[0:1, 0:1]
    lane = lax.broadcasted_iota(jnp.int32, (ROWS, HD), 1)
    other_doc = jnp.where(ids_col == first, 0.0, 1.0)
    qaug[...] = jnp.where(lane == 0, 1.0, jnp.where(lane == 1, other_doc, 0.0)).astype(jnp.bfloat16)
    t_pos = lax.broadcasted_iota(jnp.int32, (ROWS, ROWS), 0)
    s_pos = lax.broadcasted_iota(jnp.int32, (ROWS, ROWS), 1)
    seen = (wide(ids_col, 2) == ids) & (s_pos <= t_pos)
    dmask[...] = jnp.where(seen, 0.0, HIDDEN)
    kaug[HD + 16:, :] = jnp.zeros((HD - 16, 2 * ROWS), jnp.bfloat16)
    vaug[:, HD:] = jnp.ones((2 * ROWS, HD), jnp.bfloat16)

    vaug[0:HD, 0:HD] = v_ref[0:HD, :]
    vaug[HD:ROWS, 0:HD] = v_ref[HD:, :]
    q_load.wait()

    def cols(h):
        return pl.ds(pl.multiple_of(h * HD, HD), HD)

    @pl.loop(0, HEADS)
    def _(h):
        s = jnp.dot(q[:, cols(h)], own[0:HD, :], preferred_element_type=jnp.float32) + dmask[...]
        m = jnp.broadcast_to(jnp.max(s, axis=1, keepdims=True), (ROWS, HD))
        p = jnp.exp2((s - wide(m, 2)) * RATE).astype(jnp.bfloat16)
        acc[h] = jnp.dot(p, vaug[0:ROWS, :], preferred_element_type=jnp.float32)
        top[h] = m

    def fill(j, place):
        rows = pl.ds(place * ROWS, ROWS)
        msg = got.at[j - 1]
        kaug[0:HD, rows] = msg[0:HD, :]
        bias = jnp.where(msg[HD:HD + 16, :].astype(jnp.float32) == first, 0.0, HIDDEN)
        row = lax.broadcasted_iota(jnp.int32, (16, ROWS), 0)
        kaug[HD:HD + 16, rows] = jnp.where(row == 0, bias, jnp.where(row == 1, HIDDEN, 0.0)).astype(jnp.bfloat16)
        vaug[place * ROWS:place * ROWS + HD, 0:HD] = msg[HD + 16:, 0:HD]
        vaug[place * ROWS + HD:(place + 1) * ROWS, 0:HD] = msg[HD + 16:, HD:]

    def arrive(j):
        @pl.when(ctx >= j)
        def _():
            kv_copy(j).wait_recv()

        @pl.when(ctx < j)
        def _():
            got[j - 1] = jnp.full((MSG, ROWS), -1.0, jnp.bfloat16)

    def step(h, toks, n):
        left = jnp.concatenate([q[toks, cols(h)], qaug[toks, :]], axis=1)
        s = jnp.dot(left, kaug[...], preferred_element_type=jnp.float32)
        old = top[h, toks, :]
        m = jnp.maximum(old, jnp.broadcast_to(jnp.max(s, axis=1, keepdims=True), (n, HD)))
        p = jnp.exp2((s - wide(m, 4)) * RATE).astype(jnp.bfloat16)
        shrink = jnp.exp2((old - m) * RATE)
        total = acc[h, toks, :] * wide(shrink, 2) + jnp.dot(p, vaug[...], preferred_element_type=jnp.float32)
        return m, total

    for pair in range(BACK // 2):
        for place in range(2):
            j = 2 * pair + place + 1
            arrive(j)
            fill(j, place)
        if pair < BACK // 2 - 1:
            @pl.loop(0, HEADS)
            def _(h):
                m, total = step(h, pl.ds(0, ROWS), ROWS)
                top[h] = m
                acc[h] = total

    for c in w_loads:
        c.wait()

    def core_copy(i):
        return pltpu.make_async_remote_copy(
            src_ref=core_out.at[i], dst_ref=core_in.at[i], send_sem=cs_sem.at[i], recv_sem=cr_sem.at[i],
            device_id=(ctx, mate), device_id_type=MESH)

    def y_copy(i):
        return pltpu.make_async_remote_copy(
            src_ref=y_out.at[i], dst_ref=y_in.at[i], send_sem=ys_sem.at[i], recv_sem=yr_sem.at[i],
            device_id=(ctx, far), device_id_type=MESH)

    def relay(i):
        core_copy(i).wait_recv()
        y_out[i] = (keep[i, :, 0:COLS] + core_in[i, :, 0:COLS].astype(jnp.float32)).astype(jnp.bfloat16)
        y_copy(i).start()

    for i in range(CHUNKS):
        toks = pl.ds(i * TOK, TOK)

        @pl.loop(0, HEADS)
        def _(h):
            _, total = step(h, toks, TOK)
            att[:, cols(h)] = (total[:, 0:HD] / total[:, HD:]).astype(jnp.bfloat16)

        core_out[i] = jnp.dot(att[...], w[:, 0:2 * COLS], preferred_element_type=jnp.float32).astype(jnp.bfloat16)
        core_copy(i).start()
        keep[i] = jnp.dot(att[...], w[:, 2 * COLS:], preferred_element_type=jnp.float32)
        if i > 0:
            relay(i - 1)
    relay(CHUNKS - 1)

    for i in range(CHUNKS):
        y_copy(i).wait_recv()
        mine = keep[i, :, COLS:] + core_in[i, :, COLS:].astype(jnp.float32)
        o_ref[i * TOK:(i + 1) * TOK, :] = (mine + y_in[i].astype(jnp.float32)).astype(jnp.bfloat16)

    for i in range(CHUNKS):
        core_copy(i).wait_send()
        y_copy(i).wait_send()
    for j in range(1, BACK + 1):
        @pl.when(ctx + j < n_ctx)
        def _():
            kv_copy(j).wait_send()


def solution(mesh):
    n_ctx = mesh.shape["ctx"]

    def local(queries, keys, values, doc_ids, w_out):
        vmem = pl.BlockSpec(memory_space=pltpu.VMEM)
        hbm = pl.BlockSpec(memory_space=pl.ANY)
        bf16, f32 = jnp.bfloat16, jnp.float32
        return pl.pallas_call(
            functools.partial(kernel, n_ctx),
            out_shape=jax.ShapeDtypeStruct((ROWS, COLS), bf16),
            in_specs=[hbm, vmem, vmem, vmem, hbm],
            out_specs=vmem,
            scratch_shapes=[
                pltpu.VMEM((ROWS, HEADS * HD), bf16),
                pltpu.VMEM((HEADS * HD, 4 * COLS), bf16),
                pltpu.VMEM((MSG, ROWS), bf16),
                pltpu.VMEM((BACK, MSG, ROWS), bf16),
                pltpu.VMEM((2 * HD, 2 * ROWS), bf16),
                pltpu.VMEM((2 * ROWS, 2 * HD), bf16),
                pltpu.VMEM((ROWS, HD), bf16),
                pltpu.VMEM((ROWS, ROWS), f32),
                pltpu.VMEM((HEADS, ROWS, 2 * HD), f32),
                pltpu.VMEM((HEADS, ROWS, HD), f32),
                pltpu.VMEM((TOK, HEADS * HD), bf16),
                pltpu.VMEM((CHUNKS, TOK, 2 * COLS), f32),
                pltpu.VMEM((CHUNKS, TOK, 2 * COLS), bf16),
                pltpu.VMEM((CHUNKS, TOK, 2 * COLS), bf16),
                pltpu.VMEM((CHUNKS, TOK, COLS), bf16),
                pltpu.VMEM((CHUNKS, TOK, COLS), bf16),
                pltpu.SemaphoreType.DMA,
                pltpu.SemaphoreType.DMA((4,)),
                pltpu.SemaphoreType.DMA((BACK,)),
                pltpu.SemaphoreType.DMA((BACK,)),
                pltpu.SemaphoreType.DMA((CHUNKS,)),
                pltpu.SemaphoreType.DMA((CHUNKS,)),
                pltpu.SemaphoreType.DMA((CHUNKS,)),
                pltpu.SemaphoreType.DMA((CHUNKS,)),
            ],
            compiler_params=pltpu.CompilerParams(
                collective_id=0, has_side_effects=True, vmem_limit_bytes=48 * 2**20),
        )(queries, keys, values, doc_ids.reshape(1, ROWS), w_out)

    placed = (P("ctx", "head"), P("ctx", "head"), P("ctx", "head"), P("ctx"), P("head", None))
    return jax.shard_map(local, mesh=mesh, in_specs=placed, out_specs=P("ctx", "head"), check_vma=False)
```

time: 205 us -> 65.9 us (0.32)
  the two profiles are of different devices: /device:TPU:128 before, /device:TPU:198 now
where the time goes in v1:
time: 65.9 us; the launch traced here: 65.7 us
  Pallas kernels  61.6 us (93%)
  local copies, waits for them, and re-layouts  4.12 us (6%)
    pallas_call x1, Pallas kernels, local(): pl.pallas_call(functools.partial(kernel, n_ctx), out_shape=jax.ShapeDtype...  61.6 us
    unnamed x9, local copies, waits for them, and re-layouts  4.12 us

profile of v1, /device:TPU:198, one launch (start us, length us, event | category | flops | bytes accessed | tf_op | source)
XLA Modules:
  0.0 65.7 jit_solution(2546919305433188231)
XLA Ops:
  0.0 0.0 copy-start
  0.0 1.0 %copy-done = bf16[256,1024]{1,0:T(8,128)(2,1)S(1)} copy-done((bf16[256,1024]{1,0:T(8,128)(2,1)S(1)}, bf16[256,1024]{1,0:T(8,128)(2,1)}, u32[]{:S(2)}) %copy-start) | copy-done | bytes 524312
  1.0 0.0 copy-start.1
  1.0 0.8 %copy-done.1 = bf16[256,128]{1,0:T(8,128)(2,1)S(1)} copy-done((bf16[256,128]{1,0:T(8,128)(2,1)S(1)}, bf16[256,128]{1,0:T(8,128)(2,1)}, u32[]{:S(2)}) %copy-start.1) | copy-done | bytes 65560
  1.9 0.0 copy-start.2
  1.9 0.8 %copy-done.2 = bf16[256,128]{1,0:T(8,128)(2,1)S(1)} copy-done((bf16[256,128]{1,0:T(8,128)(2,1)S(1)}, bf16[256,128]{1,0:T(8,128)(2,1)}, u32[]{:S(2)}) %copy-start.2) | copy-done | bytes 65560
  2.7 0.0 copy-start.3
  2.7 0.7 %copy-done.3 = s32[256]{0:T(256)S(1)} copy-done((s32[256]{0:T(256)S(1)}, s32[256]{0:T(256)}, u32[]{:S(2)}) %copy-start.3) | copy-done | bytes 1048
  3.4 61.6 %shard_map.55 = bf16[256,640]{1,0:T(8,128)(2,1)S(1)} custom-call(bf16[256,1024]{1,0:T(8,128)(2,1)S(1)} %copy-done, bf16[256,128]{1,0:T(8,128)(2,1)S(1)} %copy-done.1, bf16[256,128]{1,0:T(8,128)(2,1)S(1)} %copy-done.2, s32[1,256]{1,0:T(1,128)S(1)} %bitcast.1, bf16[1024,2560]{1,0:T(8,128)(2,1)} %w_hbm.1), custom_call_target="tpu_custom_call" | custom-call | tf_op jit(solution)/shard_map/pallas_call | solution.py:197
  65.0 0.7 %copy.7 = bf16[256,640]{1,0:T(8,128)(2,1)} copy(bf16[256,640]{1,0:T(8,128)(2,1)S(1)} %shard_map.55) | data formatting | bytes 655360
Async XLA Ops:
  0.0 1.0 %copy-start = (bf16[256,1024]{1,0:T(8,128)(2,1)S(1)}, bf16[256,1024]{1,0:T(8,128)(2,1)}, u32[]{:S(2)}) copy-start(bf16[256,1024]{1,0:T(8,128)(2,1)} %q_hbm.1) | copy-start | bytes 1572868
  1.0 0.8 %copy-start.1 = (bf16[256,128]{1,0:T(8,128)(2,1)S(1)}, bf16[256,128]{1,0:T(8,128)(2,1)}, u32[]{:S(2)}) copy-start(bf16[256,128]{1,0:T(8,128)(2,1)} %k_ref.1) | copy-start | bytes 196612
  1.9 0.8 %copy-start.2 = (bf16[256,128]{1,0:T(8,128)(2,1)S(1)}, bf16[256,128]{1,0:T(8,128)(2,1)}, u32[]{:S(2)}) copy-start(bf16[256,128]{1,0:T(8,128)(2,1)} %v_ref.1) | copy-start | bytes 196612
  2.7 0.7 %copy-start.3 = (s32[256]{0:T(256)S(1)}, s32[256]{0:T(256)}, u32[]{:S(2)}) copy-start(s32[256]{0:T(256)} %param.8) | copy-start | bytes 3076

commit v2 on v0

v2 whole, which is shorter than its diff:
```python
import functools
import math

import jax
import jax.numpy as jnp
from jax import lax
from jax.experimental import pallas as pl
from jax.experimental.pallas import tpu as pltpu
from jax.sharding import PartitionSpec as P

MESH = pl.DeviceIdType.MESH
HD = 128
ROWS = 256
HEADS = 8
COLS = 640
HIDDEN = -1e30
RATE = math.log2(math.e) / math.sqrt(HD)
CHUNKS = 2
TOK = ROWS // CHUNKS
KEY_ROWS = HD + 16
MSG = KEY_ROWS + HD
SLOTS = 8
BEHIND, ROW, LEFT, RIGHT, ROW_LEFT, ROW_RIGHT, ACROSS, ROW_ACROSS = range(SLOTS)
RING = 4
FAR, NEAR = range(2)
PART = 256
PARTS = HEADS * TOK // PART


def wide(x, n):
    return jnp.concatenate([x] * n, axis=1)


def kernel(n_ctx, q_hbm, k_hbm, v_hbm, ids_hbm, w_hbm, o_ref,
           q, k, v, marks, w, own, got, rows, kaug, vaug, acc, top, att, keep,
           core_out, core_in, y_out, y_in,
           load_sem, w_sem, send_sem, recv_sem, cs_sem, cr_sem, ys_sem, yr_sem):
    ctx = lax.axis_index("ctx")
    head = lax.axis_index("head")
    y_hi, core = head // 2, lax.rem(head, 2)
    x = lax.rem(ctx, RING)
    base = ctx - x
    y_lo = lax.rem(ctx // RING, 2)
    upper, lower = y_lo == 0, y_lo == 1
    inner = (x == 1) | (x == 2)
    outer = jnp.logical_not(inner)
    x_right, x_left, x_over = lax.rem(x + 1, RING), lax.rem(x + RING - 1, RING), lax.rem(x + 2, RING)
    right, left, over = base + x_right, base + x_left, base + x_over
    have_behind, have_row = ctx >= 2 * RING, ctx >= RING
    give_behind, give_row = ctx + 2 * RING < n_ctx, ctx + RING < n_ctx
    mate = y_hi * 2 + (1 - core)
    far = (1 - y_hi) * 2 + core

    barrier = pltpu.get_barrier_semaphore()

    def greet(where, c, h):
        @pl.when(where)
        def _():
            pl.semaphore_signal(barrier, inc=1, device_id=(c, h), device_id_type=MESH)

    greet(have_behind, ctx - 2 * RING, head)
    for c in (x, x_left, x_right):
        greet(have_row, base - RING + c, head)
    for c, h in ((left, head), (right, head), (over, head), (ctx, mate), (ctx, far)):
        greet(True, c, h)

    loads = [pltpu.make_async_copy(src, dst, load_sem.at[i])
             for i, (src, dst) in enumerate([(k_hbm, k), (v_hbm, v), (ids_hbm, marks), (q_hbm, q)])]
    for c in loads:
        c.start()
    for c in loads[:3]:
        c.wait()

    ids = marks[...].astype(jnp.float32)
    own[0:HD, :] = k[...].T
    own[HD:HD + 16, :] = jnp.broadcast_to(ids, (16, ROWS)).astype(jnp.bfloat16)
    own[KEY_ROWS:, 0:HD] = v[0:HD, :]
    own[KEY_ROWS:, HD:] = v[HD:, :]

    greeted = 5 + give_behind.astype(jnp.int32) + 3 * give_row.astype(jnp.int32)
    pl.semaphore_wait(barrier, greeted)

    sent = []

    def send(where, src, slot, lane, dest):
        copy = pltpu.make_async_remote_copy(
            src_ref=own if src is None else got.at[src], dst_ref=got.at[slot],
            send_sem=send_sem.at[lane], recv_sem=recv_sem.at[slot],
            device_id=(dest, head), device_id_type=MESH)

        @pl.when(where)
        def _():
            copy.start()

        sent.append((where, copy))

    def arrive(slot, where):
        @pl.when(where)
        def _():
            pltpu.make_async_remote_copy(
                src_ref=own, dst_ref=got.at[slot], send_sem=send_sem.at[0],
                recv_sem=recv_sem.at[slot], device_id=(left, head), device_id_type=MESH).wait_recv()

        @pl.when(jnp.logical_not(where))
        def _():
            got[slot] = jnp.full((MSG, ROWS), -1.0, jnp.bfloat16)

    ahead, next_base = lax.rem(ctx + 2 * RING, n_ctx), lax.rem(base + RING, n_ctx)
    send(give_behind, None, BEHIND, 0, ahead)
    send(give_row, None, ROW, 1, next_base + x)
    send(x < RING - 1, None, LEFT, 2, right)
    send(x == 0, None, RIGHT, 3, left)

    w_loads = []
    groups = [(1 - y_hi) * 2 + (1 - core), (1 - y_hi) * 2 + core, y_hi * 2 + (1 - core), y_hi * 2 + core]
    for i, g in enumerate(groups):
        c = pltpu.make_async_copy(
            w_hbm.at[:, pl.ds(pl.multiple_of(g * COLS, 128), COLS)], w.at[:, pl.ds(i * COLS, COLS)], w_sem.at[i])
        c.start()
        w_loads.append(c)

    ids_col = jnp.broadcast_to(ids, (HD, ROWS)).T
    first = ids[0:1, 0:1]
    lane = lax.broadcasted_iota(jnp.int32, (ROWS, HD), 1)
    other_doc = jnp.where(ids_col == first, 0.0, 1.0)
    qaug = jnp.where(lane == 0, 1.0, jnp.where(lane == 1, other_doc, 0.0)).astype(jnp.bfloat16)
    t_pos = lax.broadcasted_iota(jnp.int32, (ROWS, ROWS), 0)
    s_pos = lax.broadcasted_iota(jnp.int32, (ROWS, ROWS), 1)
    seen = (wide(ids_col, 2) == ids) & (s_pos <= t_pos)
    dmask = jnp.where(seen, 0.0, HIDDEN)
    kaug[:, HD + 16:, :] = jnp.zeros((2, HD - 16, 2 * ROWS), jnp.bfloat16)
    vaug[:, :, HD:] = jnp.ones((2, 2 * ROWS, HD), jnp.bfloat16)
    vaug[1, 0:HD, 0:HD] = v[0:HD, :]
    vaug[1, HD:ROWS, 0:HD] = v[HD:, :]

    loads[3].wait()
    for c in range(CHUNKS):
        for h in range(HEADS):
            at = (c * HEADS + h) * TOK
            rows[at:at + TOK, 0:HD] = q[c * TOK:(c + 1) * TOK, h * HD:(h + 1) * HD]
            rows[at:at + TOK, HD:] = qaug[c * TOK:(c + 1) * TOK, :]

    for c in range(CHUNKS):
        seen_keys = (c + 1) * TOK
        mask = jnp.concatenate([dmask[c * TOK:(c + 1) * TOK, 0:seen_keys]] * (PART // TOK), axis=0)
        for i in range(c * PARTS, (c + 1) * PARTS):
            here = pl.ds(i * PART, PART)
            s = jnp.dot(rows[here, 0:HD], own[0:HD, 0:seen_keys], preferred_element_type=jnp.float32) + mask
            m = jnp.broadcast_to(jnp.max(s, axis=1, keepdims=True), (PART, HD))
            p = jnp.exp2((s - wide(m, seen_keys // HD)) * RATE).astype(jnp.bfloat16)
            acc[here, :] = jnp.dot(p, vaug[1, 0:seen_keys, :], preferred_element_type=jnp.float32)
            top[here, :] = m

    def fill(slot, b, place):
        cols = pl.ds(place * ROWS, ROWS)
        msg = got.at[slot]
        kaug[b, 0:HD, cols] = msg[0:HD, :]
        bias = jnp.where(msg[HD:HD + 16, :].astype(jnp.float32) == first, 0.0, HIDDEN)
        row = lax.broadcasted_iota(jnp.int32, (16, ROWS), 0)
        kaug[b, HD:HD + 16, cols] = jnp.where(row == 0, bias, jnp.where(row == 1, HIDDEN, 0.0)).astype(jnp.bfloat16)
        vaug[b, place * ROWS:place * ROWS + HD, 0:HD] = msg[KEY_ROWS:, 0:HD]
        vaug[b, place * ROWS + HD:(place + 1) * ROWS, 0:HD] = msg[KEY_ROWS:, HD:]

    def step(here, b):
        s = jnp.dot(rows[here, :], kaug[b], preferred_element_type=jnp.float32)
        old = top[here, :]
        m = jnp.maximum(old, jnp.broadcast_to(jnp.max(s, axis=1, keepdims=True), (PART, HD)))
        p = jnp.exp2((s - wide(m, 4)) * RATE).astype(jnp.bfloat16)
        shrink = jnp.exp2((old - m) * RATE)
        total = acc[here, :] * wide(shrink, 2) + jnp.dot(p, vaug[b], preferred_element_type=jnp.float32)
        return m, total

    def fold(b):
        for i in range(CHUNKS * PARTS):
            here = pl.ds(i * PART, PART)
            m, total = step(here, b)
            top[here, :] = m
            acc[here, :] = total

    arrive(BEHIND, have_behind)
    send(have_behind & (x > 0), BEHIND, RIGHT, 4, left)
    send(have_behind & (x == RING - 1), BEHIND, LEFT, 5, right)
    arrive(ROW, have_row)
    send(have_row, ROW, ROW_LEFT, 6, right)
    send(have_row, ROW, ROW_RIGHT, 7, left)
    arrive(LEFT, have_behind | (x > 0))
    send(inner, LEFT, ACROSS, 8, right)
    fill(BEHIND, 0, 0)
    fill(ROW, 0, 1)
    fold(0)
    arrive(RIGHT, have_behind | (x == RING - 1))
    send(inner & have_behind, RIGHT, ACROSS, 9, left)
    arrive(ROW_LEFT, have_row)
    send(outer & have_row, ROW_LEFT, ROW_ACROSS, 10, right)
    arrive(ROW_RIGHT, have_row)
    send(outer & have_row, ROW_RIGHT, ROW_ACROSS, 11, left)
    fill(LEFT, 1, 0)
    fill(ROW_LEFT, 1, 1)
    fold(1)
    fill(RIGHT, 0, 0)
    fill(ROW_RIGHT, 0, 1)
    fold(0)
    arrive(ACROSS, have_behind | (x > 1))
    arrive(ROW_ACROSS, have_row)
    fill(ACROSS, 1, 0)
    fill(ROW_ACROSS, 1, 1)

    for c in w_loads:
        c.wait()

    def core_copy(side, c):
        return pltpu.make_async_remote_copy(
            src_ref=core_out.at[side, c], dst_ref=core_in.at[side, c], send_sem=cs_sem.at[side, c],
            recv_sem=cr_sem.at[side, c], device_id=(ctx, mate), device_id_type=MESH)

    def y_copy(c):
        return pltpu.make_async_remote_copy(
            src_ref=y_out.at[c], dst_ref=y_in.at[c], send_sem=ys_sem.at[c], recv_sem=yr_sem.at[c],
            device_id=(ctx, far), device_id_type=MESH)

    def finish(c):
        for i in range(PARTS):
            _, total = step(pl.ds((c * PARTS + i) * PART, PART), 1)
            mean = (total[:, 0:HD] / total[:, HD:]).astype(jnp.bfloat16)
            for n in range(PART // TOK):
                h = i * (PART // TOK) + n
                att[c, :, h * HD:(h + 1) * HD] = mean[n * TOK:(n + 1) * TOK, :]

    def project(side, c):
        at = 2 * side * COLS
        core_out[side, c] = jnp.dot(
            att[c], w[:, at:at + COLS], preferred_element_type=jnp.float32).astype(jnp.bfloat16)
        core_copy(side, c).start()
        keep[side, c] = jnp.dot(att[c], w[:, at + COLS:at + 2 * COLS], preferred_element_type=jnp.float32)

    def relay(c):
        core_copy(FAR, c).wait_recv()
        y_out[c] = (keep[FAR, c] + core_in[FAR, c].astype(jnp.float32)).astype(jnp.bfloat16)
        y_copy(c).start()

    finish(0)
    project(FAR, 0)
    finish(1)
    relay(0)
    project(FAR, 1)
    project(NEAR, 0)
    relay(1)
    project(NEAR, 1)

    for c in range(CHUNKS):
        core_copy(NEAR, c).wait_recv()
        keep[NEAR, c] += core_in[NEAR, c].astype(jnp.float32)
    for c in range(CHUNKS):
        y_copy(c).wait_recv()
        o_ref[c * TOK:(c + 1) * TOK, :] = (keep[NEAR, c] + y_in[c].astype(jnp.float32)).astype(jnp.bfloat16)

    for c in range(CHUNKS):
        core_copy(FAR, c).wait_send()
        core_copy(NEAR, c).wait_send()
        y_copy(c).wait_send()
    for where, copy in sent:
        @pl.when(where)
        def _():
            copy.wait_send()


def solution(mesh):
    n_ctx = mesh.shape["ctx"]

    def local(queries, keys, values, doc_ids, w_out):
        hbm = pl.BlockSpec(memory_space=pltpu.HBM)
        bf16, f32 = jnp.bfloat16, jnp.float32
        vmem, dma = pltpu.VMEM, pltpu.SemaphoreType.DMA
        return pl.pallas_call(
            functools.partial(kernel, n_ctx),
            out_shape=pltpu.VMEM((ROWS, COLS), bf16),
            in_specs=[hbm] * 5,
            out_specs=pl.BlockSpec(memory_space=pltpu.VMEM),
            scratch_shapes=[
                vmem((ROWS, HEADS * HD), bf16),
                vmem((ROWS, HD), bf16),
                vmem((ROWS, HD), bf16),
                vmem((1, ROWS), jnp.int32),
                vmem((HEADS * HD, 4 * COLS), bf16),
                vmem((MSG, ROWS), bf16),
                vmem((SLOTS, MSG, ROWS), bf16),
                vmem((HEADS * ROWS, 2 * HD), bf16),
                vmem((2, 2 * HD, 2 * ROWS), bf16),
                vmem((2, 2 * ROWS, 2 * HD), bf16),
                vmem((HEADS * ROWS, 2 * HD), f32),
                vmem((HEADS * ROWS, HD), f32),
                vmem((CHUNKS, TOK, HEADS * HD), bf16),
                vmem((2, CHUNKS, TOK, COLS), f32),
                vmem((2, CHUNKS, TOK, COLS), bf16),
                vmem((2, CHUNKS, TOK, COLS), bf16),
                vmem((CHUNKS, TOK, COLS), bf16),
                vmem((CHUNKS, TOK, COLS), bf16),
                dma((4,)),
                dma((4,)),
                dma((12,)),
                dma((SLOTS,)),
                dma((2, CHUNKS)),
                dma((2, CHUNKS)),
                dma((CHUNKS,)),
                dma((CHUNKS,)),
            ],
            compiler_params=pltpu.CompilerParams(
                collective_id=0, has_side_effects=True, vmem_limit_bytes=63 * 2**20),
        )(queries, keys, values, doc_ids.reshape(1, ROWS), w_out)

    placed = (P("ctx", "head"), P("ctx", "head"), P("ctx", "head"), P("ctx"), P("head", None))
    return jax.shard_map(local, mesh=mesh, in_specs=placed, out_specs=P("ctx", "head"), check_vma=False)
```

time: 205 us -> 37.1 us (0.18); the launches traced: 201 us -> 37 us
  waiting for transfers between devices: 94.5 us -> 0 us
  starting transfers between devices: 50.1 us -> 0 us
  Pallas kernels: 0 us -> 36.3 us
  matrix products: 19.1 us -> 0 us
  local copies, waits for them, and re-layouts: 16.1 us -> 0.73 us
  between operations: 13.5 us -> 0.01 us
  other arithmetic: 6.8 us -> 0 us
    ppermute x24 -> x0, waiting for transfers between devices: 56.6 us -> none  [from_behind(): return lax.ppermute(block, axis, route)]
    ppermute x24 -> x0, starting transfers between devices: 50.1 us -> none  [from_behind(): return lax.ppermute(block, axis, route)]
    unnamed x2 -> x0, waiting for transfers between devices: 37.8 us -> none
    pallas_call x0 -> x1, Pallas kernels: none -> 36.3 us  [local(): pl.pallas_call(functools.partial(kernel, n_ctx), out_shape=pltpu.VMEM((RO...]
    dot_general x19 -> x0, matrix products: 19.1 us -> none  [the longest x9 9.83 us: attend(): jnp.einsum('kgts,skd->kgtd', weights.astype(jnp.bfloat16), value_rows, pr...]
    while x65 -> x0, local copies, waits for them, and re-layouts: 9.58 us -> none
    unnamed x7 -> x1, local copies, waits for them, and re-layouts: 6.53 us -> 0.73 us
    reduce_sum x9 -> x0, other arithmetic: 4.63 us -> none  [attend(): run_sum = run_sum * factor + jnp.sum(weights, axis=-1)]
  transfers between devices with their start and end apart: 25 -> 0, of which waited for: 24 -> 0; matrix products, arithmetic and copies ran while one was open for 5% -> 0% of each run, Pallas kernels for 0% -> 0%
where the time goes in v2:
time: 37.1 us; the launch traced here: 37 us
  Pallas kernels  36.3 us (98%)
  local copies, waits for them, and re-layouts  0.73 us (2%)
    pallas_call x1, Pallas kernels, local(): pl.pallas_call(functools.partial(kernel, n_ctx), out_shape=pltpu.VMEM((RO...  36.3 us

profile of v2, /device:TPU:128, one launch (start us, length us, event | category | flops | bytes accessed | tf_op | source)
XLA Modules:
  0.0 37.0 jit_solution(6990654607811947495)
XLA Ops:
  0.0 36.3 %shard_map.55 = bf16[256,640]{1,0:T(8,128)(2,1)S(1)} custom-call(bf16[256,1024]{1,0:T(8,128)(2,1)} %q_hbm.1, bf16[256,128]{1,0:T(8,128)(2,1)} %k_hbm.1, bf16[256,128]{1,0:T(8,128)(2,1)} %v_hbm.1, s32[1,256]{1,0:T(1,128)} %bitcast.1, bf16[1024,2560]{1,0:T(8,128)(2,1)} %w_hbm.1), custom_call_target="tpu_custom_call" | custom-call | tf_op jit(solution)/shard_map/pallas_call | solution.py:274
  36.3 0.7 %copy.7 = bf16[256,640]{1,0:T(8,128)(2,1)} copy(bf16[256,640]{1,0:T(8,128)(2,1)S(1)} %shard_map.55) | data formatting | bytes 655360

commit v3 on v2

v3 whole, which is shorter than its diff:
```python
import functools
import math

import jax
import jax.numpy as jnp
from jax import lax
from jax.experimental import pallas as pl
from jax.experimental.pallas import tpu as pltpu
from jax.sharding import PartitionSpec as P

MESH = pl.DeviceIdType.MESH
HD = 128
ROWS = 256
HEADS = 8
COLS = 640
HIDDEN = -1e30
RATE = math.log2(math.e) / math.sqrt(HD)
CHUNKS = ((0, 64), (64, 64), (128, 128))
KEY_ROWS = HD + 16
MSG = KEY_ROWS + HD
SLOTS = 8
BEHIND, ROW, LEFT, RIGHT, ROW_LEFT, ROW_RIGHT, ACROSS, ROW_ACROSS = range(SLOTS)
PASS_LEFT, PASS_RIGHT = SLOTS, SLOTS + 1
RING = 4
FAR, NEAR = range(2)
PART = 256


def wide(x, n):
    return jnp.concatenate([x] * n, axis=1)


def kernel(n_ctx, q_hbm, k_hbm, v_hbm, ids_hbm, w_hbm, o_ref,
           q, k, v, marks, w, own, got, rows, kaug, vaug, acc, top, att, keep,
           core_out, core_in, y_out, y_in,
           load_sem, w_sem, send_sem, recv_sem, cs_sem, cr_sem, ys_sem, yr_sem):
    ctx = lax.axis_index("ctx")
    head = lax.axis_index("head")
    y_hi, core = head // 2, lax.rem(head, 2)
    x = lax.rem(ctx, RING)
    base = ctx - x
    inner = (x == 1) | (x == 2)
    outer = jnp.logical_not(inner)
    right, left = base + lax.rem(x + 1, RING), base + lax.rem(x + RING - 1, RING)
    have_behind, have_row = ctx >= 2 * RING, ctx >= RING
    give_behind, give_row = ctx + 2 * RING < n_ctx, ctx + RING < n_ctx
    mate = y_hi * 2 + (1 - core)
    far = (1 - y_hi) * 2 + core

    barrier = pltpu.get_barrier_semaphore()

    def greet(where, c, h):
        @pl.when(where)
        def _():
            pl.semaphore_signal(barrier, inc=1, device_id=(c, h), device_id_type=MESH)

    greet(have_behind, ctx - 2 * RING, head)
    greet(have_row, ctx - RING, head)
    for c, h in ((left, head), (right, head), (ctx, mate), (ctx, far)):
        greet(True, c, h)

    loads = [pltpu.make_async_copy(src, dst, load_sem.at[i])
             for i, (src, dst) in enumerate([(k_hbm, k), (v_hbm, v), (ids_hbm, marks), (q_hbm, q)])]
    for c in loads:
        c.start()
    for c in loads[:3]:
        c.wait()

    ids = marks[...].astype(jnp.float32)
    own[0:HD, :] = k[...].T
    own[HD:HD + 16, :] = jnp.broadcast_to(ids, (16, ROWS)).astype(jnp.bfloat16)
    own[KEY_ROWS:, 0:HD] = v[0:HD, :]
    own[KEY_ROWS:, HD:] = v[HD:, :]

    greeted = 4 + give_behind.astype(jnp.int32) + give_row.astype(jnp.int32)
    pl.semaphore_wait(barrier, greeted)

    sent = []

    def send(where, src, slot, lane, dest):
        copy = pltpu.make_async_remote_copy(
            src_ref=own if src is None else got.at[src], dst_ref=got.at[slot],
            send_sem=send_sem.at[lane], recv_sem=recv_sem.at[slot],
            device_id=(dest, head), device_id_type=MESH)

        @pl.when(where)
        def _():
            copy.start()

        sent.append((where, copy))

    def arrive(slot, where):
        @pl.when(where)
        def _():
            pltpu.make_async_remote_copy(
                src_ref=own, dst_ref=got.at[slot], send_sem=send_sem.at[0],
                recv_sem=recv_sem.at[slot], device_id=(left, head), device_id_type=MESH).wait_recv()

    def blank(slot, where):
        @pl.when(where)
        def _():
            got[slot] = jnp.full((MSG, ROWS), -1.0, jnp.bfloat16)

    for slot in (BEHIND, RIGHT, LEFT, ACROSS):
        here = {RIGHT: x < RING - 1, LEFT: x == 0, ACROSS: x < 2}.get(slot, True)
        blank(slot, jnp.logical_not(have_behind) & here)
    for slot in (ROW, ROW_LEFT, ROW_RIGHT, ROW_ACROSS):
        blank(slot, jnp.logical_not(have_row))

    ahead, below = lax.rem(ctx + 2 * RING, n_ctx), lax.rem(ctx + RING, n_ctx)
    send(give_row, None, ROW, 0, below)
    send((x > 0) & give_behind, None, PASS_RIGHT, 1, left)
    send(x < RING - 1, None, LEFT, 2, right)
    send((x == RING - 1) & give_behind, None, PASS_LEFT, 3, right)
    send(x == 0, None, RIGHT, 4, left)

    w_loads = []
    groups = [(1 - y_hi) * 2 + (1 - core), (1 - y_hi) * 2 + core, y_hi * 2 + (1 - core), y_hi * 2 + core]
    for i, g in enumerate(groups):
        c = pltpu.make_async_copy(
            w_hbm.at[:, pl.ds(pl.multiple_of(g * COLS, 128), COLS)], w.at[:, pl.ds(i * COLS, COLS)], w_sem.at[i])
        c.start()
        w_loads.append(c)

    ids_col = jnp.broadcast_to(ids, (HD, ROWS)).T
    first = ids[0:1, 0:1]
    lane = lax.broadcasted_iota(jnp.int32, (ROWS, HD), 1)
    other_doc = jnp.where(ids_col == first, 0.0, 1.0)
    qaug = jnp.where(lane == 0, 1.0, jnp.where(lane == 1, other_doc, 0.0)).astype(jnp.bfloat16)
    t_pos = lax.broadcasted_iota(jnp.int32, (ROWS, ROWS), 0)
    s_pos = lax.broadcasted_iota(jnp.int32, (ROWS, ROWS), 1)
    seen = (wide(ids_col, 2) == ids) & (s_pos <= t_pos)
    dmask = jnp.where(seen, 0.0, HIDDEN)
    kaug[:, HD + 16:, :] = jnp.zeros((2, HD - 16, 2 * ROWS), jnp.bfloat16)
    vaug[:, :, HD:] = jnp.ones((2, 2 * ROWS, HD), jnp.bfloat16)
    vaug[1, 0:HD, 0:HD] = v[0:HD, :]
    vaug[1, HD:ROWS, 0:HD] = v[HD:, :]

    loads[3].wait()
    for t, n in CHUNKS:
        for h in range(HEADS):
            at = t * HEADS + h * n
            rows[at:at + n, 0:HD] = q[t:t + n, h * HD:(h + 1) * HD]
            rows[at:at + n, HD:] = qaug[t:t + n, :]

    for t, n in CHUNKS:
        seen_keys = -(-(t + n) // HD) * HD
        mask = jnp.concatenate([dmask[t:t + n, 0:seen_keys]] * (PART // n), axis=0)
        for at in range(t * HEADS, (t + n) * HEADS, PART):
            here = pl.ds(at, PART)
            s = jnp.dot(rows[here, 0:HD], own[0:HD, 0:seen_keys], preferred_element_type=jnp.float32) + mask
            m = jnp.broadcast_to(jnp.max(s, axis=1, keepdims=True), (PART, HD))
            p = jnp.exp2((s - wide(m, seen_keys // HD)) * RATE).astype(jnp.bfloat16)
            acc[here, :] = jnp.dot(p, vaug[1, 0:seen_keys, :], preferred_element_type=jnp.float32)
            top[here, :] = m

    def fill(slot, b, place):
        cols = pl.ds(place * ROWS, ROWS)
        msg = got.at[slot]
        kaug[b, 0:HD, cols] = msg[0:HD, :]
        bias = jnp.where(msg[HD:HD + 16, :].astype(jnp.float32) == first, 0.0, HIDDEN)
        row = lax.broadcasted_iota(jnp.int32, (16, ROWS), 0)
        kaug[b, HD:HD + 16, cols] = jnp.where(row == 0, bias, jnp.where(row == 1, HIDDEN, 0.0)).astype(jnp.bfloat16)
        vaug[b, place * ROWS:place * ROWS + HD, 0:HD] = msg[KEY_ROWS:, 0:HD]
        vaug[b, place * ROWS + HD:(place + 1) * ROWS, 0:HD] = msg[KEY_ROWS:, HD:]

    def step(here, b, keys):
        s = jnp.dot(rows[here, :], kaug[b, :, 0:keys], preferred_element_type=jnp.float32)
        old = top[here, :]
        m = jnp.maximum(old, jnp.broadcast_to(jnp.max(s, axis=1, keepdims=True), (PART, HD)))
        p = jnp.exp2((s - wide(m, keys // HD)) * RATE).astype(jnp.bfloat16)
        shrink = jnp.exp2((old - m) * RATE)
        total = acc[here, :] * wide(shrink, 2) + jnp.dot(p, vaug[b, 0:keys, :], preferred_element_type=jnp.float32)
        return m, total

    def fold(b, keys=2 * ROWS):
        for at in range(0, HEADS * ROWS, PART):
            here = pl.ds(at, PART)
            m, total = step(here, b, keys)
            top[here, :] = m
            acc[here, :] = total

    send(give_behind, None, BEHIND, 5, ahead)
    arrive(ROW, have_row)
    send(have_row, ROW, ROW_LEFT, 8, right)
    send(have_row, ROW, ROW_RIGHT, 9, left)
    arrive(PASS_RIGHT, (x < RING - 1) & give_behind)
    send((x < RING - 1) & give_behind, PASS_RIGHT, RIGHT, 6, ahead)
    arrive(PASS_LEFT, (x == 0) & give_behind)
    send((x == 0) & give_behind, PASS_LEFT, LEFT, 7, ahead)
    arrive(LEFT, x > 0)
    send(inner, LEFT, ACROSS, 10, right)
    arrive(BEHIND, have_behind)
    fill(BEHIND, 0, 0)
    fill(ROW, 0, 1)
    fold(0)
    arrive(ROW_LEFT, outer & have_row)
    send(outer & have_row, ROW_LEFT, ROW_ACROSS, 12, right)
    arrive(ROW_RIGHT, outer & have_row)
    send(outer & have_row, ROW_RIGHT, ROW_ACROSS, 13, left)
    arrive(RIGHT, inner & have_behind)
    send(inner & have_behind, RIGHT, ACROSS, 11, left)
    arrive(LEFT, (x == 0) & have_behind)
    arrive(RIGHT, (x == RING - 1) | ((x == 0) & have_behind))
    fill(LEFT, 1, 0)
    fill(RIGHT, 1, 1)
    fold(1)
    arrive(ROW_LEFT, inner & have_row)
    arrive(ROW_RIGHT, inner & have_row)
    fill(ROW_LEFT, 0, 0)
    fill(ROW_RIGHT, 0, 1)
    fold(0)
    arrive(ACROSS, have_behind | (x > 1))
    fill(ACROSS, 1, 0)
    fold(1, ROWS)
    arrive(ROW_ACROSS, have_row)
    fill(ROW_ACROSS, 0, 0)

    for c in w_loads:
        c.wait()

    def core_copy(side, c):
        t, n = CHUNKS[c] if side == FAR else (0, ROWS)
        part = pl.ds(t, n)
        return pltpu.make_async_remote_copy(
            src_ref=core_out.at[side, part], dst_ref=core_in.at[side, part], send_sem=cs_sem.at[side, c],
            recv_sem=cr_sem.at[side, c], device_id=(ctx, mate), device_id_type=MESH)

    def y_copy(c):
        t, n = CHUNKS[c]
        part = pl.ds(t, n)
        return pltpu.make_async_remote_copy(
            src_ref=y_out.at[part], dst_ref=y_in.at[part], send_sem=ys_sem.at[c], recv_sem=yr_sem.at[c],
            device_id=(ctx, far), device_id_type=MESH)

    def finish(c):
        t, n = CHUNKS[c]
        for at in range(t * HEADS, (t + n) * HEADS, PART):
            _, total = step(pl.ds(at, PART), 0, ROWS)
            mean = (total[:, 0:HD] / total[:, HD:]).astype(jnp.bfloat16)
            for i in range(PART // n):
                h = (at - t * HEADS) // n + i
                att[t:t + n, h * HD:(h + 1) * HD] = mean[i * n:(i + 1) * n, :]

    def give(side, c):
        t, n = CHUNKS[c] if side == FAR else (0, ROWS)
        at = 2 * side * COLS
        core_out[side, t:t + n, :] = jnp.dot(
            att[t:t + n, :], w[:, at:at + COLS], preferred_element_type=jnp.float32).astype(jnp.bfloat16)
        core_copy(side, c).start()

    def hold(side, c):
        t, n = CHUNKS[c] if side == FAR else (0, ROWS)
        at = (2 * side + 1) * COLS
        keep[side, t:t + n, :] = jnp.dot(att[t:t + n, :], w[:, at:at + COLS], preferred_element_type=jnp.float32)

    def relay(c):
        t, n = CHUNKS[c]
        core_copy(FAR, c).wait_recv()
        y_out[t:t + n, :] = (keep[FAR, t:t + n, :] + core_in[FAR, t:t + n, :].astype(jnp.float32)).astype(jnp.bfloat16)
        y_copy(c).start()

    finish(0)
    give(FAR, 0)
    hold(FAR, 0)
    finish(1)
    give(FAR, 1)
    hold(FAR, 1)
    relay(0)
    finish(2)
    relay(1)
    give(FAR, 2)
    hold(FAR, 2)
    give(NEAR, 0)
    hold(NEAR, 0)
    relay(2)
    core_copy(NEAR, 0).wait_recv()
    keep[NEAR] += core_in[NEAR].astype(jnp.float32)
    for c, (t, n) in enumerate(CHUNKS):
        y_copy(c).wait_recv()
        o_ref[t:t + n, :] = (keep[NEAR, t:t + n, :] + y_in[t:t + n, :].astype(jnp.float32)).astype(jnp.bfloat16)

    core_copy(NEAR, 0).wait_send()
    for c in range(len(CHUNKS)):
        core_copy(FAR, c).wait_send()
        y_copy(c).wait_send()
    for where, copy in sent:
        @pl.when(where)
        def _():
            copy.wait_send()


def solution(mesh):
    n_ctx = mesh.shape["ctx"]

    def local(queries, keys, values, doc_ids, w_out):
        hbm = pl.BlockSpec(memory_space=pltpu.HBM)
        bf16, f32 = jnp.bfloat16, jnp.float32
        vmem, dma = pltpu.VMEM, pltpu.SemaphoreType.DMA
        return pl.pallas_call(
            functools.partial(kernel, n_ctx),
            out_shape=pltpu.VMEM((ROWS, COLS), bf16),
            in_specs=[hbm] * 5,
            out_specs=pl.BlockSpec(memory_space=pltpu.VMEM),
            scratch_shapes=[
                vmem((ROWS, HEADS * HD), bf16),
                vmem((ROWS, HD), bf16),
                vmem((ROWS, HD), bf16),
                vmem((1, ROWS), jnp.int32),
                vmem((HEADS * HD, 4 * COLS), bf16),
                vmem((MSG, ROWS), bf16),
                vmem((SLOTS + 2, MSG, ROWS), bf16),
                vmem((HEADS * ROWS, 2 * HD), bf16),
                vmem((2, 2 * HD, 2 * ROWS), bf16),
                vmem((2, 2 * ROWS, 2 * HD), bf16),
                vmem((HEADS * ROWS, 2 * HD), f32),
                vmem((HEADS * ROWS, HD), f32),
                vmem((ROWS, HEADS * HD), bf16),
                vmem((2, ROWS, COLS), f32),
                vmem((2, ROWS, COLS), bf16),
                vmem((2, ROWS, COLS), bf16),
                vmem((ROWS, COLS), bf16),
                vmem((ROWS, COLS), bf16),
                dma((4,)),
                dma((4,)),
                dma((14,)),
                dma((SLOTS + 2,)),
                dma((2, len(CHUNKS))),
                dma((2, len(CHUNKS))),
                dma((len(CHUNKS),)),
                dma((len(CHUNKS),)),
            ],
            compiler_params=pltpu.CompilerParams(
                collective_id=0, has_side_effects=True, vmem_limit_bytes=63 * 2**20),
        )(queries, keys, values, doc_ids.reshape(1, ROWS), w_out)

    placed = (P("ctx", "head"), P("ctx", "head"), P("ctx", "head"), P("ctx"), P("head", None))
    return jax.shard_map(local, mesh=mesh, in_specs=placed, out_specs=P("ctx", "head"), check_vma=False)
```

time: 37.1 us -> 34.7 us (0.935)
  Pallas kernels: 36.3 us -> 33.9 us
    pallas_call x1, Pallas kernels: 36.3 us -> 33.9 us  [local(): pl.pallas_call(functools.partial(kernel, n_ctx), out_shape=pltpu.VMEM((RO...]
where the time goes in v3:
time: 34.7 us
  Pallas kernels  33.9 us (98%)
  local copies, waits for them, and re-layouts  0.73 us (2%)
    pallas_call x1, Pallas kernels, local(): pl.pallas_call(functools.partial(kernel, n_ctx), out_shape=pltpu.VMEM((RO...  33.9 us
    unnamed x1, local copies, waits for them, and re-layouts  0.73 us

profile of v3, /device:TPU:128, one launch (start us, length us, event | category | flops | bytes accessed | tf_op | source)
XLA Modules:
  0.0 34.7 jit_solution(10605088224182404194)
XLA Ops:
  0.0 33.9 %shard_map.55 = bf16[256,640]{1,0:T(8,128)(2,1)S(1)} custom-call(bf16[256,1024]{1,0:T(8,128)(2,1)} %q_hbm.1, bf16[256,128]{1,0:T(8,128)(2,1)} %k_hbm.1, bf16[256,128]{1,0:T(8,128)(2,1)} %v_hbm.1, s32[1,256]{1,0:T(1,128)} %bitcast.1, bf16[1024,2560]{1,0:T(8,128)(2,1)} %w_hbm.1), custom_call_target="tpu_custom_call" | custom-call | tf_op jit(solution)/shard_map/pallas_call | solution.py:300
  33.9 0.7 %copy.7 = bf16[256,640]{1,0:T(8,128)(2,1)} copy(bf16[256,640]{1,0:T(8,128)(2,1)S(1)} %shard_map.55) | data formatting | bytes 655360

commit v4 on v3

--- a/solution.py
+++ b/solution.py
@@ -18,9 +18,10 @@
 CHUNKS = ((0, 64), (64, 64), (128, 128))
 KEY_ROWS = HD + 16
 MSG = KEY_ROWS + HD
+WHOLE, UPPER, LOWER = (0, MSG), (0, KEY_ROWS), (KEY_ROWS, HD)
 SLOTS = 8
 BEHIND, ROW, LEFT, RIGHT, ROW_LEFT, ROW_RIGHT, ACROSS, ROW_ACROSS = range(SLOTS)
-PASS_LEFT, PASS_RIGHT = SLOTS, SLOTS + 1
+PASS_LEFT, PASS_RIGHT, SPLIT = SLOTS, SLOTS + 1, SLOTS + 2
 RING = 4
 FAR, NEAR = range(2)
 PART = 256
@@ -40,7 +41,6 @@
     x = lax.rem(ctx, RING)
     base = ctx - x
     inner = (x == 1) | (x == 2)
-    outer = jnp.logical_not(inner)
     right, left = base + lax.rem(x + 1, RING), base + lax.rem(x + RING - 1, RING)
     have_behind, have_row = ctx >= 2 * RING, ctx >= RING
     give_behind, give_row = ctx + 2 * RING < n_ctx, ctx + RING < n_ctx
@@ -77,10 +77,12 @@
 
     sent = []
 
-    def send(where, src, slot, lane, dest):
+    def send(where, src, slot, lane, dest, part=WHOLE, flag=None):
+        flag = slot if flag is None else flag
+        part = pl.ds(*part)
         copy = pltpu.make_async_remote_copy(
-            src_ref=own if src is None else got.at[src], dst_ref=got.at[slot],
-            send_sem=send_sem.at[lane], recv_sem=recv_sem.at[slot],
+            src_ref=own.at[part] if src is None else got.at[src, part], dst_ref=got.at[slot, part],
+            send_sem=send_sem.at[lane], recv_sem=recv_sem.at[flag],
             device_id=(dest, head), device_id_type=MESH)
 
         @pl.when(where)
@@ -89,12 +91,15 @@
 
         sent.append((where, copy))
 
-    def arrive(slot, where):
+    def arrive(slot, where, part=WHOLE, flag=None):
+        flag = slot if flag is None else flag
+        part = pl.ds(*part)
+
         @pl.when(where)
         def _():
             pltpu.make_async_remote_copy(
-                src_ref=own, dst_ref=got.at[slot], send_sem=send_sem.at[0],
-                recv_sem=recv_sem.at[slot], device_id=(left, head), device_id_type=MESH).wait_recv()
+                src_ref=own.at[part], dst_ref=got.at[slot, part], send_sem=send_sem.at[0],
+                recv_sem=recv_sem.at[flag], device_id=(left, head), device_id_type=MESH).wait_recv()
 
     def blank(slot, where):
         @pl.when(where)
@@ -165,16 +170,16 @@
         vaug[b, place * ROWS + HD:(place + 1) * ROWS, 0:HD] = msg[KEY_ROWS:, HD:]
 
     def step(here, b, keys):
-        s = jnp.dot(rows[here, :], kaug[b, :, 0:keys], preferred_element_type=jnp.float32)
+        s = jnp.dot(rows[here, :], kaug[b, :, keys[0]:keys[1]], preferred_element_type=jnp.float32)
         old = top[here, :]
         m = jnp.maximum(old, jnp.broadcast_to(jnp.max(s, axis=1, keepdims=True), (PART, HD)))
-        p = jnp.exp2((s - wide(m, keys // HD)) * RATE).astype(jnp.bfloat16)
+        p = jnp.exp2((s - wide(m, (keys[1] - keys[0]) // HD)) * RATE).astype(jnp.bfloat16)
         shrink = jnp.exp2((old - m) * RATE)
-        total = acc[here, :] * wide(shrink, 2) + jnp.dot(p, vaug[b, 0:keys, :], preferred_element_type=jnp.float32)
+        total = acc[here, :] * wide(shrink, 2) + jnp.dot(p, vaug[b, keys[0]:keys[1], :], preferred_element_type=jnp.float32)
         return m, total
 
-    def fold(b, keys=2 * ROWS):
-        for at in range(0, HEADS * ROWS, PART):
+    def fold(b, keys=(0, 2 * ROWS), upto=HEADS * ROWS):
+        for at in range(0, upto, PART):
             here = pl.ds(at, PART)
             m, total = step(here, b, keys)
             top[here, :] = m
@@ -194,10 +199,10 @@
     fill(BEHIND, 0, 0)
     fill(ROW, 0, 1)
     fold(0)
-    arrive(ROW_LEFT, outer & have_row)
-    send(outer & have_row, ROW_LEFT, ROW_ACROSS, 12, right)
-    arrive(ROW_RIGHT, outer & have_row)
-    send(outer & have_row, ROW_RIGHT, ROW_ACROSS, 13, left)
+    arrive(ROW_LEFT, have_row)
+    send(have_row, ROW_LEFT, ROW_ACROSS, 12, right, UPPER)
+    arrive(ROW_RIGHT, have_row)
+    send(have_row, ROW_RIGHT, ROW_ACROSS, 13, left, LOWER, SPLIT)
     arrive(RIGHT, inner & have_behind)
     send(inner & have_behind, RIGHT, ACROSS, 11, left)
     arrive(LEFT, (x == 0) & have_behind)
@@ -205,16 +210,14 @@
     fill(LEFT, 1, 0)
     fill(RIGHT, 1, 1)
     fold(1)
-    arrive(ROW_LEFT, inner & have_row)
-    arrive(ROW_RIGHT, inner & have_row)
     fill(ROW_LEFT, 0, 0)
     fill(ROW_RIGHT, 0, 1)
     fold(0)
     arrive(ACROSS, have_behind | (x > 1))
     fill(ACROSS, 1, 0)
-    fold(1, ROWS)
-    arrive(ROW_ACROSS, have_row)
-    fill(ROW_ACROSS, 0, 0)
+    arrive(ROW_ACROSS, have_row, UPPER)
+    arrive(ROW_ACROSS, have_row, LOWER, SPLIT)
+    fill(ROW_ACROSS, 1, 1)
 
     for c in w_loads:
         c.wait()
@@ -236,7 +239,7 @@
     def finish(c):
         t, n = CHUNKS[c]
         for at in range(t * HEADS, (t + n) * HEADS, PART):
-            _, total = step(pl.ds(at, PART), 0, ROWS)
+            _, total = step(pl.ds(at, PART), 1, (0, 2 * ROWS))
             mean = (total[:, 0:HD] / total[:, HD:]).astype(jnp.bfloat16)
             for i in range(PART // n):
                 h = (at - t * HEADS) // n + i
@@ -324,7 +327,7 @@
                 dma((4,)),
                 dma((4,)),
                 dma((14,)),
-                dma((SLOTS + 2,)),
+                dma((SLOTS + 3,)),
                 dma((2, len(CHUNKS))),
                 dma((2, len(CHUNKS))),
                 dma((len(CHUNKS),)),

time: 34.7 us -> 33.9 us (0.977)
  Pallas kernels: 33.9 us -> 33.1 us
    pallas_call x1, Pallas kernels: 33.9 us -> 33.1 us  [local(): pl.pallas_call(functools.partial(kernel, n_ctx), out_shape=pltpu.VMEM((RO...]
where the time goes in v4:
time: 33.9 us; the launch traced here: 33.8 us
  Pallas kernels  33.1 us (98%)
  local copies, waits for them, and re-layouts  0.73 us (2%)
    pallas_call x1, Pallas kernels, local(): pl.pallas_call(functools.partial(kernel, n_ctx), out_shape=pltpu.VMEM((RO...  33.1 us
    unnamed x1, local copies, waits for them, and re-layouts  0.73 us

profile of v4, /device:TPU:128, one launch (start us, length us, event | category | flops | bytes accessed | tf_op | source)
XLA Modules:
  0.0 33.8 jit_solution(6406994988510764974)
XLA Ops:
  0.0 33.1 %shard_map.55 = bf16[256,640]{1,0:T(8,128)(2,1)S(1)} custom-call(bf16[256,1024]{1,0:T(8,128)(2,1)} %q_hbm.1, bf16[256,128]{1,0:T(8,128)(2,1)} %k_hbm.1, bf16[256,128]{1,0:T(8,128)(2,1)} %v_hbm.1, s32[1,256]{1,0:T(1,128)} %bitcast.1, bf16[1024,2560]{1,0:T(8,128)(2,1)} %w_hbm.1), custom_call_target="tpu_custom_call" | custom-call | tf_op jit(solution)/shard_map/pallas_call | solution.py:303
  33.1 0.7 %copy.7 = bf16[256,640]{1,0:T(8,128)(2,1)} copy(bf16[256,640]{1,0:T(8,128)(2,1)S(1)} %shard_map.55) | data formatting | bytes 655360

commit v5 on v4

--- a/solution.py
+++ b/solution.py
@@ -199,12 +199,12 @@
     fill(BEHIND, 0, 0)
     fill(ROW, 0, 1)
     fold(0)
+    arrive(RIGHT, inner & have_behind)
+    send(inner & have_behind, RIGHT, ACROSS, 11, left)
     arrive(ROW_LEFT, have_row)
     send(have_row, ROW_LEFT, ROW_ACROSS, 12, right, UPPER)
     arrive(ROW_RIGHT, have_row)
     send(have_row, ROW_RIGHT, ROW_ACROSS, 13, left, LOWER, SPLIT)
-    arrive(RIGHT, inner & have_behind)
-    send(inner & have_behind, RIGHT, ACROSS, 11, left)
     arrive(LEFT, (x == 0) & have_behind)
     arrive(RIGHT, (x == RING - 1) | ((x == 0) & have_behind))
     fill(LEFT, 1, 0)

time: 33.9 us -> 33.3 us (0.982)
  Pallas kernels: 33.1 us -> 32.4 us
    pallas_call x1, Pallas kernels: 33.1 us -> 32.4 us  [local(): pl.pallas_call(functools.partial(kernel, n_ctx), out_shape=pltpu.VMEM((RO...]
where the time goes in v5:
time: 33.3 us; the launch traced here: 33.2 us
  Pallas kernels  32.4 us (97%)
  local copies, waits for them, and re-layouts  0.73 us (2%)
    pallas_call x1, Pallas kernels, local(): pl.pallas_call(functools.partial(kernel, n_ctx), out_shape=pltpu.VMEM((RO...  32.4 us
    unnamed x1, local copies, waits for them, and re-layouts  0.73 us

profile of v5, /device:TPU:128, one launch (start us, length us, event | category | flops | bytes accessed | tf_op | source)
XLA Modules:
  0.0 33.2 jit_solution(2051663042873177558)
XLA Ops:
  0.0 32.4 %shard_map.55 = bf16[256,640]{1,0:T(8,128)(2,1)S(1)} custom-call(bf16[256,1024]{1,0:T(8,128)(2,1)} %q_hbm.1, bf16[256,128]{1,0:T(8,128)(2,1)} %k_hbm.1, bf16[256,128]{1,0:T(8,128)(2,1)} %v_hbm.1, s32[1,256]{1,0:T(1,128)} %bitcast.1, bf16[1024,2560]{1,0:T(8,128)(2,1)} %w_hbm.1), custom_call_target="tpu_custom_call" | custom-call | tf_op jit(solution)/shard_map/pallas_call | solution.py:303
  32.4 0.7 %copy.7 = bf16[256,640]{1,0:T(8,128)(2,1)} copy(bf16[256,640]{1,0:T(8,128)(2,1)S(1)} %shard_map.55) | data formatting | bytes 655360

commit v6 on v5

--- a/solution.py
+++ b/solution.py
@@ -119,6 +119,7 @@
     send((x == RING - 1) & give_behind, None, PASS_LEFT, 3, right)
     send(x == 0, None, RIGHT, 4, left)
 
+    send(give_behind & (lax.rem(ctx // RING, 2) == 1), None, BEHIND, 5, ahead)
     w_loads = []
     groups = [(1 - y_hi) * 2 + (1 - core), (1 - y_hi) * 2 + core, y_hi * 2 + (1 - core), y_hi * 2 + core]
     for i, g in enumerate(groups):
@@ -185,7 +186,7 @@
             top[here, :] = m
             acc[here, :] = total
 
-    send(give_behind, None, BEHIND, 5, ahead)
+    send(give_behind & (lax.rem(ctx // RING, 2) == 0), None, BEHIND, 5, ahead)
     arrive(ROW, have_row)
     send(have_row, ROW, ROW_LEFT, 8, right)
     send(have_row, ROW, ROW_RIGHT, 9, left)

time: 33.3 us -> 33.3 us (level)
  no operation moved by 1% of the time
where the time goes in v6:
time: 33.3 us; the launch traced here: 33.2 us
  Pallas kernels  32.4 us (97%)
  local copies, waits for them, and re-layouts  0.73 us (2%)
    pallas_call x1, Pallas kernels, local(): pl.pallas_call(functools.partial(kernel, n_ctx), out_shape=pltpu.VMEM((RO...  32.4 us
    unnamed x1, local copies, waits for them, and re-layouts  0.73 us

profile of v6, /device:TPU:128, one launch (start us, length us, event | category | flops | bytes accessed | tf_op | source)
XLA Modules:
  0.0 33.2 jit_solution(8564013577078442657)
XLA Ops:
  0.0 32.4 %shard_map.55 = bf16[256,640]{1,0:T(8,128)(2,1)S(1)} custom-call(bf16[256,1024]{1,0:T(8,128)(2,1)} %q_hbm.1, bf16[256,128]{1,0:T(8,128)(2,1)} %k_hbm.1, bf16[256,128]{1,0:T(8,128)(2,1)} %v_hbm.1, s32[1,256]{1,0:T(1,128)} %bitcast.1, bf16[1024,2560]{1,0:T(8,128)(2,1)} %w_hbm.1), custom_call_target="tpu_custom_call" | custom-call | tf_op jit(solution)/shard_map/pallas_call | solution.py:304
  32.4 0.7 %copy.7 = bf16[256,640]{1,0:T(8,128)(2,1)} copy(bf16[256,640]{1,0:T(8,128)(2,1)S(1)} %shard_map.55) | data formatting | bytes 655360
